TPU v7x, 32 devices: a whole 2x2x4 slice. The times are simulated.
32 devices in a mesh: clip: 8 (over z, x), seq: 4 (over y, core).
Axes of the slice: x: 2, y: 2, z: 4, core: 2. Of those that a mesh axis runs over, the one named last changes fastest.
Arguments:
- frames: bfloat16 [8, 1024, 768], P('clip', 'seq'), may hold values from -6 to 6
- out_grad: bfloat16 [8, 1024, 768], P('clip', 'seq'), may hold values from -6 to 6
- attn_in: bfloat16 [2, 768, 2304], P(None, ('clip', 'seq')), may hold values from -0.21875 to 0.21875
- attn_out: bfloat16 [2, 768, 768], P(None, ('clip', 'seq')), may hold values from -3.5 to 3.5
- mlp_in: bfloat16 [2, 768, 3072], P(None, ('clip', 'seq')), may hold values from -0.21875 to 0.21875
- mlp_out: bfloat16 [2, 3072, 768], P(None, ('clip', 'seq')), may hold values from -0.109375 to 0.109375
- norm_gains: bfloat16 [2, 2, 768], P(None, None, ('clip', 'seq')), may hold values from 0.25 to 1.75
- shifts: bfloat16 [2, 6, 768], P(None, None, ('clip', 'seq')), may hold values from -3 to 3
- mlp_bias: bfloat16 [2, 3072], P(None, ('clip', 'seq')), may hold values from -3 to 3
Outputs:
- encoded: bfloat16 [8, 1024, 768], P('clip', 'seq')
- frames_grad: float32 [8, 1024, 768], P('clip', 'seq')
- attn_in_grad: float32 [2, 768, 2304], P(None, ('clip', 'seq'))
- attn_out_grad: float32 [2, 768, 768], P(None, ('clip', 'seq'))
- mlp_in_grad: float32 [2, 768, 3072], P(None, ('clip', 'seq'))
- mlp_out_grad: float32 [2, 3072, 768], P(None, ('clip', 'seq'))
- norm_gains_grad: float32 [2, 2, 768], P(None, None, ('clip', 'seq'))
- shifts_grad: float32 [2, 6, 768], P(None, None, ('clip', 'seq'))
- mlp_bias_grad: float32 [2, 3072], P(None, ('clip', 'seq'))
All inputs are finite; a program needn't handle non-finite values.
Results may differ from a plain program's by a relative error of at most 0.015.
Values may be sent and summed in bfloat16 or wider, within the bound.
A program may use at most 192 MiB of HBM per device.

v0:
```python
import jax
import jax.numpy as jnp
from jax import lax
from jax.sharding import PartitionSpec as P

D = 768
H = 12
HD = 64


eps_norm = 1e-05
root_half = 0.7071067811865476
inv_root_two_pi = 0.3989422804014327


def product(left, right):
    return jnp.dot(left, right, preferred_element_type=jnp.float32)


def product_left(left, right):
    return lax.dot_general(
        left, right, (((0,), (0,)), ((), ())), preferred_element_type=jnp.float32
    )


def product_right(left, right):
    return lax.dot_general(
        left, right, (((1,), (1,)), ((), ())), preferred_element_type=jnp.float32
    )


def norm_forward(rows, gain, shift):
    center = rows - jnp.mean(rows, axis=1, keepdims=True)
    inv_scale = lax.rsqrt(jnp.mean(center * center, axis=1, keepdims=True) + eps_norm)
    unit_rows = center * inv_scale
    return (unit_rows * gain + shift, unit_rows, inv_scale)


def norm_backward(upstream, unit_rows, inv_scale, gain):
    scaled = upstream * gain
    mean_plain = jnp.mean(scaled, axis=1, keepdims=True)
    mean_unit = jnp.mean(scaled * unit_rows, axis=1, keepdims=True)
    back = inv_scale * (scaled - mean_plain - unit_rows * mean_unit)
    return (back, jnp.sum(upstream * unit_rows, axis=0), jnp.sum(upstream, axis=0))


def gelu_slope(pre_gelu):
    cumulative = 0.5 * (1.0 + lax.erf(pre_gelu * root_half))
    density = jnp.exp(-0.5 * pre_gelu * pre_gelu) * inv_root_two_pi
    return cumulative + pre_gelu * density


def to_heads(clip_rows):
    groups, count = (clip_rows.shape[0], clip_rows.shape[1])
    return clip_rows.reshape(groups, count, H, HD).transpose(2, 0, 1, 3)


def from_heads(heads):
    groups, count = (heads.shape[1], heads.shape[2])
    return heads.transpose(1, 2, 0, 3).reshape(groups * count, H * HD)


def column_sums(rows):
    return jnp.sum(rows.astype(jnp.float32), axis=0)


def seq_major(term, position):
    clip_count = lax.axis_size("clip")
    seq_count = lax.axis_size("seq")
    shape = term.shape
    split_shape = (
        shape[:position]
        + (clip_count, seq_count, shape[position] // (clip_count * seq_count))
        + shape[position + 1 :]
    )
    return jnp.swapaxes(term.reshape(split_shape), position, position + 1).reshape(shape)


def attend_forward(queries, all_keys, all_values):
    score_scale = HD ** (-0.5)

    def one_head(operands):
        query_head, key_head, value_head = operands
        scores = (
            jnp.einsum("gqd,gkd->gqk", query_head, key_head, preferred_element_type=jnp.float32)
            * score_scale
        )
        row_max = jnp.max(scores, axis=2, keepdims=True)
        row_total = jnp.sum(jnp.exp(scores - row_max), axis=2, keepdims=True)
        log_total = row_max + jnp.log(row_total)
        attn_probs = jnp.exp(scores - log_total).astype(jnp.bfloat16)
        outputs = jnp.einsum(
            "gqk,gkd->gqd", attn_probs, value_head, preferred_element_type=jnp.float32
        )
        return (outputs, log_total[:, :, 0])

    outputs, log_total = lax.map(
        one_head, (to_heads(queries), to_heads(all_keys), to_heads(all_values))
    )
    return (from_heads(outputs), log_total)


def attend_backward(queries, all_keys, all_values, log_total, grad_attended):
    score_scale = HD ** (-0.5)

    def one_head(operands):
        query_head, key_head, value_head, total_head, grad_head = operands
        scores = (
            jnp.einsum("gqd,gkd->gqk", query_head, key_head, preferred_element_type=jnp.float32)
            * score_scale
        )
        attn_probs = jnp.exp(scores - total_head[:, :, None])
        grad_probs = jnp.einsum(
            "gqd,gkd->gqk", grad_head, value_head, preferred_element_type=jnp.float32
        )
        inner_sum = jnp.sum(grad_probs * attn_probs, axis=2, keepdims=True)
        grad_scores = (attn_probs * (grad_probs - inner_sum)).astype(jnp.bfloat16)
        grad_values = jnp.einsum(
            "gqk,gqd->gkd",
            attn_probs.astype(jnp.bfloat16),
            grad_head,
            preferred_element_type=jnp.float32,
        )
        grad_queries = (
            jnp.einsum("gqk,gkd->gqd", grad_scores, key_head, preferred_element_type=jnp.float32)
            * score_scale
        )
        grad_keys = (
            jnp.einsum("gqk,gqd->gkd", grad_scores, query_head, preferred_element_type=jnp.float32)
            * score_scale
        )
        return (grad_queries, grad_keys, grad_values)

    heads = lax.map(
        one_head,
        (
            to_heads(queries),
            to_heads(all_keys),
            to_heads(all_values),
            log_total,
            to_heads(grad_attended),
        ),
    )
    groups = queries.shape[0]
    grad_queries = from_heads(heads[0])
    grad_keys = from_heads(heads[1]).reshape(groups, -1, H * HD)
    grad_values = from_heads(heads[2]).reshape(groups, -1, H * HD)
    return (grad_queries, grad_keys, grad_values)


def unpack_weights(weights):
    w_attn_in, w_attn_out, w_mlp_in, w_mlp_out, gain_rows, shift_rows, bias_mlp = weights
    return (
        w_attn_in,
        w_attn_out,
        w_mlp_in,
        w_mlp_out,
        gain_rows.astype(jnp.float32),
        shift_rows.astype(jnp.float32),
        bias_mlp.astype(jnp.float32),
    )


def layer_forward(residual, weights, groups):
    w_attn_in, w_attn_out, w_mlp_in, w_mlp_out, gain_rows, shift_rows, bias_mlp = unpack_weights(
        weights
    )
    normed = norm_forward(residual, gain_rows[0], shift_rows[0])[0].astype(jnp.bfloat16)
    qkv_bias = jnp.concatenate([shift_rows[1], jnp.zeros_like(shift_rows[1]), shift_rows[2]])
    projected = (product(normed, w_attn_in) + qkv_bias).astype(jnp.bfloat16)
    queries = projected[:, :D].reshape(groups, -1, D)
    local_keys = projected[:, D : 2 * D].reshape(groups, -1, D)
    local_values = projected[:, 2 * D :].reshape(groups, -1, D)
    all_keys, all_values = (
        lax.all_gather(local_keys, "seq", axis=1, tiled=True),
        lax.all_gather(local_values, "seq", axis=1, tiled=True),
    )
    attended, log_total = attend_forward(queries, all_keys, all_values)
    attended = attended.astype(jnp.bfloat16)
    middle = residual + product(attended, w_attn_out) + shift_rows[3]
    normed_two = norm_forward(middle, gain_rows[1], shift_rows[4])[0].astype(jnp.bfloat16)
    pre_gelu = product(normed_two, w_mlp_in) + bias_mlp
    hidden = jax.nn.gelu(pre_gelu, approximate=False).astype(jnp.bfloat16)
    result = middle + product(hidden, w_mlp_out) + shift_rows[5]
    saved_layer = (
        residual,
        normed,
        queries,
        all_keys,
        all_values,
        log_total,
        attended,
        middle,
        normed_two,
    )
    return (result, saved_layer)


def layer_backward(upstream, saved_layer, weights, groups):
    w_attn_in, w_attn_out, w_mlp_in, w_mlp_out, gain_rows, shift_rows, bias_mlp = unpack_weights(
        weights
    )
    residual, normed, queries, all_keys, all_values, log_total, attended, middle, normed_two = (
        saved_layer
    )
    pre_gelu = product(normed_two, w_mlp_in) + bias_mlp
    hidden = jax.nn.gelu(pre_gelu, approximate=False).astype(jnp.bfloat16)
    upstream_low = upstream.astype(jnp.bfloat16)
    grad_mlp_out = product_left(hidden, upstream_low)
    grad_bias_two = column_sums(upstream_low)
    grad_pre = (product_right(upstream_low, w_mlp_out) * gelu_slope(pre_gelu)).astype(jnp.bfloat16)
    grad_mlp_in = product_left(normed_two, grad_pre)
    grad_mlp_bias = column_sums(grad_pre)
    grad_normed_two = product_right(grad_pre, w_mlp_in)
    unit_two, scale_two = norm_forward(middle, gain_rows[1], shift_rows[4])[1:]
    back_two, grad_gain_two, grad_shift_two = norm_backward(
        grad_normed_two, unit_two, scale_two, gain_rows[1]
    )
    grad_middle = upstream + back_two
    middle_low = grad_middle.astype(jnp.bfloat16)
    grad_attn_out = product_left(attended, middle_low)
    grad_bias_out = column_sums(middle_low)
    grad_attended = (
        product_right(middle_low, w_attn_out).astype(jnp.bfloat16).reshape(groups, -1, D)
    )
    grad_queries, key_terms, value_terms = attend_backward(
        queries, all_keys, all_values, log_total, grad_attended
    )
    grad_keys, grad_values = (
        lax.psum_scatter(
            key_terms.astype(jnp.bfloat16), "seq", scatter_dimension=1, tiled=True
        ).astype(jnp.float32),
        lax.psum_scatter(
            value_terms.astype(jnp.bfloat16), "seq", scatter_dimension=1, tiled=True
        ).astype(jnp.float32),
    )
    rows = grad_queries.shape[0]
    grad_projected = jnp.concatenate(
        [grad_queries, grad_keys.reshape(rows, D), grad_values.reshape(rows, D)], axis=1
    ).astype(jnp.bfloat16)
    grad_attn_in = product_left(normed, grad_projected)
    projected_sums = column_sums(grad_projected)
    grad_normed = product_right(grad_projected, w_attn_in)
    unit_one, scale_one = norm_forward(residual, gain_rows[0], shift_rows[0])[1:]
    back_one, grad_gain_one, grad_shift_one = norm_backward(
        grad_normed, unit_one, scale_one, gain_rows[0]
    )
    grad_residual = grad_middle + back_one
    grad_gains = jnp.stack([grad_gain_one, grad_gain_two])
    grad_shifts = jnp.stack(
        [
            grad_shift_one,
            projected_sums[:D],
            projected_sums[2 * D :],
            grad_bias_out,
            grad_shift_two,
            grad_bias_two,
        ]
    )
    grad_terms = (
        grad_attn_in,
        grad_attn_out,
        grad_mlp_in,
        grad_mlp_out,
        grad_gains,
        grad_shifts,
        grad_mlp_bias,
    )
    return (grad_residual, grad_terms)


def body(frames, out_grad, attn_in, attn_out, mlp_in, mlp_out, norm_gains, shifts, mlp_bias):
    layers = attn_in.shape[0]
    groups, frame_count, width = frames.shape
    residual = frames.astype(jnp.float32).reshape(groups * frame_count, width)
    kept_weights = []
    saved_all = []
    for layer_index in range(layers):
        weights = (
            lax.all_gather(attn_in[layer_index], ("clip", "seq"), axis=0, tiled=True),
            lax.all_gather(attn_out[layer_index], ("clip", "seq"), axis=0, tiled=True),
            lax.all_gather(mlp_in[layer_index], ("clip", "seq"), axis=0, tiled=True),
            lax.all_gather(mlp_out[layer_index], ("clip", "seq"), axis=0, tiled=True),
            lax.all_gather(norm_gains[layer_index], ("clip", "seq"), axis=1, tiled=True),
            lax.all_gather(shifts[layer_index], ("clip", "seq"), axis=1, tiled=True),
            lax.all_gather(mlp_bias[layer_index], ("clip", "seq"), axis=0, tiled=True),
        )
        kept_weights.append(weights)
        residual, saved_layer = layer_forward(residual, weights, groups)
        saved_all.append(saved_layer)
    encoded = residual.astype(jnp.bfloat16).reshape(groups, frame_count, width)
    upstream = out_grad.astype(jnp.float32).reshape(groups * frame_count, width)
    shards = [None] * layers
    layer_dims = (0, 0, 0, 0, 1, 1, 0)
    for layer_index in reversed(range(layers)):
        weights = (
            lax.all_gather(attn_in[layer_index], ("clip", "seq"), axis=0, tiled=True),
            lax.all_gather(attn_out[layer_index], ("clip", "seq"), axis=0, tiled=True),
            lax.all_gather(mlp_in[layer_index], ("clip", "seq"), axis=0, tiled=True),
            lax.all_gather(mlp_out[layer_index], ("clip", "seq"), axis=0, tiled=True),
            lax.all_gather(norm_gains[layer_index], ("clip", "seq"), axis=1, tiled=True),
            lax.all_gather(shifts[layer_index], ("clip", "seq"), axis=1, tiled=True),
            lax.all_gather(mlp_bias[layer_index], ("clip", "seq"), axis=0, tiled=True),
        )
        upstream, grad_terms = layer_backward(upstream, saved_all[layer_index], weights, groups)
        ordered = [seq_major(grad_terms[position], layer_dims[position]) for position in range(7)]
        halves = (
            lax.psum_scatter(
                ordered[0].astype(jnp.bfloat16), "seq", scatter_dimension=0, tiled=True
            ).astype(jnp.float32),
            lax.psum_scatter(
                ordered[1].astype(jnp.bfloat16), "seq", scatter_dimension=0, tiled=True
            ).astype(jnp.float32),
            lax.psum_scatter(
                ordered[2].astype(jnp.bfloat16), "seq", scatter_dimension=0, tiled=True
            ).astype(jnp.float32),
            lax.psum_scatter(
                ordered[3].astype(jnp.bfloat16), "seq", scatter_dimension=0, tiled=True
            ).astype(jnp.float32),
            lax.psum_scatter(
                ordered[4].astype(jnp.bfloat16), "seq", scatter_dimension=1, tiled=True
            ).astype(jnp.float32),
            lax.psum_scatter(
                ordered[5].astype(jnp.bfloat16), "seq", scatter_dimension=1, tiled=True
            ).astype(jnp.float32),
            lax.psum_scatter(
                ordered[6].astype(jnp.bfloat16), "seq", scatter_dimension=0, tiled=True
            ).astype(jnp.float32),
        )
        shards[layer_index] = (
            lax.psum_scatter(halves[0], "clip", scatter_dimension=0, tiled=True),
            lax.psum_scatter(halves[1], "clip", scatter_dimension=0, tiled=True),
            lax.psum_scatter(halves[2], "clip", scatter_dimension=0, tiled=True),
            lax.psum_scatter(halves[3], "clip", scatter_dimension=0, tiled=True),
            lax.psum_scatter(halves[4], "clip", scatter_dimension=1, tiled=True),
            lax.psum_scatter(halves[5], "clip", scatter_dimension=1, tiled=True),
            lax.psum_scatter(halves[6], "clip", scatter_dimension=0, tiled=True),
        )
    outputs = tuple(
        (jnp.stack([layer_shard[position] for layer_shard in shards]) for position in range(7))
    )
    frames_grad = upstream.reshape(groups, frame_count, width)
    return (
        encoded,
        frames_grad,
        outputs[0],
        outputs[1],
        outputs[2],
        outputs[3],
        outputs[4],
        outputs[5],
        outputs[6],
    )


def solution(mesh):
    return jax.shard_map(
        body,
        mesh=mesh,
        in_specs=(
            P("clip", "seq", None),
            P("clip", "seq", None),
            P(None, ("clip", "seq"), None),
            P(None, ("clip", "seq"), None),
            P(None, ("clip", "seq"), None),
            P(None, ("clip", "seq"), None),
            P(None, None, ("clip", "seq")),
            P(None, None, ("clip", "seq")),
            P(None, ("clip", "seq")),
        ),
        out_specs=(
            P("clip", "seq", None),
            P("clip", "seq", None),
            P(None, ("clip", "seq"), None),
            P(None, ("clip", "seq"), None),
            P(None, ("clip", "seq"), None),
            P(None, ("clip", "seq"), None),
            P(None, None, ("clip", "seq")),
            P(None, None, ("clip", "seq")),
            P(None, ("clip", "seq")),
        ),
        check_vma=False,
    )
```

profile of v0, /device:TPU:0, one launch (start us, length us, event | category | flops | bytes accessed | tf_op | source)
XLA Modules:
  0.0 2046.1 jit_solution(11103206626811591038)
XLA Ops:
  9.8 44.7 %all-gather.10 = bf16[1,6,768]{1,0,2:T(2,128)(2,1)S(1)} all-gather(bf16[1,6,24]{1,0,2:T(2,128)(2,1)S(1)} %copy.250), channel_id=12, replica_groups=mesh['clip'=8,'seq'=4] {'clip','seq'}, dimensions={2}, use_global_device_ids=true | all-gather | bytes 9504 | tf_op jit(solution)/shard_map/all_gather | solution.py:285
  55.1 38.4 %all-gather.1 = bf16[1,6,768]{1,0,2:T(2,128)(2,1)S(1)} all-gather(bf16[1,6,24]{1,0,2:T(2,128)(2,1)S(1)} %copy.248), channel_id=3, replica_groups=mesh['clip'=8,'seq'=4] {'clip','seq'}, dimensions={2}, use_global_device_ids=true | all-gather | bytes 9504 | tf_op jit(solution)/shard_map/all_gather | solution.py:285
  94.7 38.5 %all-gather = bf16[1,2,768]{1,0,2:T(2,128)(2,1)S(1)} all-gather(bf16[1,2,24]{1,0,2:T(2,128)(2,1)S(1)} %copy.247), channel_id=2, replica_groups=mesh['clip'=8,'seq'=4] {'clip','seq'}, dimensions={2}, use_global_device_ids=true | all-gather | bytes 3168 | tf_op jit(solution)/shard_map/all_gather | solution.py:284
  175.1 37.3 %all-reduce.11 = (bf16[3072]{0:T(1024)(128)(2,1)S(1)}, bf16[3072]{0:T(1024)(128)(2,1)}) all-reduce(bf16[3072]{0:T(1024)(128)(2,1)S(1)} %dynamic-update-slice, bf16[3072]{0:T(1024)(128)(2,1)S(1)} %dynamic-update-slice.1), channel_id=9, replica_groups=mesh['clip'=8,'seq'=4] {'clip','seq'}, use_global_device_ids=true, to_apply=%add | all-reduce | flops 6144 | bytes 24576
  213.1 42.5 %all-gather.9 = bf16[1,2,768]{1,0,2:T(2,128)(2,1)S(1)} all-gather(bf16[1,2,24]{1,0,2:T(2,128)(2,1)S(1)} %copy.249), channel_id=11, replica_groups=mesh['clip'=8,'seq'=4] {'clip','seq'}, dimensions={2}, use_global_device_ids=true | all-gather | bytes 3168 | tf_op jit(solution)/shard_map/all_gather | solution.py:284
  276.4 48.4 %while.52 = (s32[]{:T(128)}, bf16[12,1,256,64]{2,3,1,0:T(8,128)(2,1)}, f32[12,1,256]{2,1,0:T(1,128)}, bf16[12,1,256,64]{3,2,1,0:T(8,128)(2,1)}, bf16[12,1,1024,6...) while((s32[]{:T(128)}, bf16[12,1,256,64]{2,3,1,0:T(8,128)(2,1)}, ...), condition=%wide.region_5.6_spmd, body=%wide.region_2.5_spmd.sunk | while | flops 68681472 | bytes 3812441 | solution.py:97
  343.6 54.5 %all-gather.41.cloned.1.call-done = bf16[1,3072,768]{2,1,0:T(8,128)(2,1)} async-done(((bf16[1,96,768]{2,1,0:T(8,128)(2,1)}), bf16[1,3072,768]{2,1,0:T(8,128)(2,1)}) %all-gather.41.cloned.1.call-update) | async-done | bytes 4718608 | tf_op jit(solution)/shard_map/all_gather | solution.py:283
  404.3 55.7 %all-gather.43.cloned.1.call-done = bf16[1,768,2304]{2,1,0:T(8,128)(2,1)} async-done(((bf16[1,24,2304]{2,1,0:T(8,128)(2,1)}), bf16[1,768,2304]{2,1,0:T(8,128)(2,1)}) %all-gather.43.cloned.1.call-update) | async-done | bytes 3538960 | tf_op jit(solution)/shard_map/all_gather | solution.py:280
  513.0 50.2 %while.53 = (s32[]{:T(128)}, bf16[12,1,256,64]{2,3,1,0:T(8,128)(2,1)}, f32[12,1,256]{2,1,0:T(1,128)}, bf16[12,1,256,64]{3,2,1,0:T(8,128)(2,1)}, bf16[12,1,1024,6...) while((s32[]{:T(128)}, bf16[12,1,256,64]{2,3,1,0:T(8,128)(2,1)}, ...), condition=%wide.region_13.14_spmd, body=%wide.region_10.13_spmd.sunk | while | flops 68681472 | bytes 3812441 | solution.py:97
  567.1 60.9 %all-gather.51.cloned.1.call-done = bf16[1,768,3072]{2,1,0:T(8,128)(2,1)} async-done(((bf16[1,24,3072]{2,1,0:T(8,128)(2,1)}), bf16[1,768,3072]{2,1,0:T(8,128)(2,1)}) %all-gather.51.cloned.1.call-update) | async-done | bytes 4718608 | tf_op jit(solution)/shard_map/all_gather | solution.py:282
  639.4 53.9 %all-gather.53.cloned.1.call-done = bf16[1,3072,768]{2,1,0:T(8,128)(2,1)} async-done(((bf16[1,96,768]{2,1,0:T(8,128)(2,1)}), bf16[1,3072,768]{2,1,0:T(8,128)(2,1)}) %all-gather.53.cloned.1.call-update) | async-done | bytes 4718608 | tf_op jit(solution)/shard_map/all_gather | solution.py:283
  710.0 105.2 %while.54 = (s32[]{:T(128)}, bf16[12,1,256,64]{2,3,1,0:T(8,128)(2,1)}, bf16[12,1,1024,64]{2,3,1,0:T(8,128)(2,1)}, bf16[12,1,1024,64]{2,3,1,0:T(8,128)(2,1)}, bf1...) while((s32[]{:T(128)}, ...), condition=%wide.region_20.21_spmd, body=%wide.region_18.20_spmd.sunk | while | flops 169950976 | bytes 9447537 | solution.py:134
  815.8 26.5 %reduce-scatter.39.cloned.1.call-done = bf16[1,256,768]{1,2,0:T(8,128)(2,1)} async-done(((bf16[1,1024,768]{1,2,0:T(8,128)(2,1)}), bf16[1,256,768]{1,2,0:T(8,128)(2,1)}) %reduce-scatter.39.cloned.1.call-update) | async-done | bytes 393232 | tf_op jit(solution)/shard_map/reduce_scatter | solution.py:233
  842.3 30.8 %reduce-scatter.37.cloned.1.call-done = bf16[1,256,768]{1,2,0:T(8,128)(2,1)} async-done(((bf16[1,1024,768]{1,2,0:T(8,128)(2,1)}), bf16[1,256,768]{1,2,0:T(8,128)(2,1)}) %reduce-scatter.37.cloned.1.call-update) | async-done | bytes 393232 | tf_op jit(solution)/shard_map/reduce_scatter | solution.py:230
  895.4 91.9 %while.55 = (s32[]{:T(128)}, bf16[12,1,256,64]{2,3,1,0:T(8,128)(2,1)}, bf16[12,1,1024,64]{2,3,1,0:T(8,128)(2,1)}, bf16[12,1,1024,64]{2,3,1,0:T(8,128)(2,1)}, bf1...) while((s32[]{:T(128)}, ...), condition=%wide.region_29.30_spmd, body=%wide.region_27.29_spmd.sunk | while | flops 169950976 | bytes 9447537 | solution.py:134
  1018.3 30.8 %reduce-scatter.41.cloned.1.call-done = bf16[1,256,768]{2,1,0:T(8,128)(2,1)} async-done(((bf16[1,1024,768]{2,1,0:T(8,128)(2,1)}), bf16[1,256,768]{2,1,0:T(8,128)(2,1)}) %reduce-scatter.41.cloned.1.call-update) | async-done | bytes 393232 | tf_op jit(solution)/shard_map/reduce_scatter | solution.py:230
  1107.4 41.1 %reduce-scatter.49.cloned.1.call-done = bf16[192,2304]{1,0:T(8,128)(2,1)} async-done(((bf16[768,2304]{1,0:T(8,128)(2,1)}), bf16[192,2304]{1,0:T(8,128)(2,1)}) %reduce-scatter.49.cloned.1.call-update) | async-done | bytes 884752 | tf_op jit(solution)/shard_map/reduce_scatter | solution.py:308
  1151.2 40.5 %reduce-scatter.45.cloned.1.call-done = bf16[192,2304]{1,0:T(8,128)(2,1)} async-done(((bf16[768,2304]{1,0:T(8,128)(2,1)}), bf16[192,2304]{1,0:T(8,128)(2,1)}) %reduce-scatter.45.cloned.1.call-update) | async-done | bytes 884752 | tf_op jit(solution)/shard_map/reduce_scatter | solution.py:308
  1194.2 47.8 %reduce-scatter.65.cloned.1.call-done = bf16[192,3072]{1,0:T(8,128)(2,1)} async-done(((bf16[768,3072]{1,0:T(8,128)(2,1)}), bf16[192,3072]{1,0:T(8,128)(2,1)}) %reduce-scatter.65.cloned.1.call-update) | async-done | bytes 1179664 | tf_op jit(solution)/shard_map/reduce_scatter | solution.py:314
  1245.1 47.5 %reduce-scatter.61.cloned.1.call-done = bf16[192,3072]{1,0:T(8,128)(2,1)} async-done(((bf16[768,3072]{1,0:T(8,128)(2,1)}), bf16[192,3072]{1,0:T(8,128)(2,1)}) %reduce-scatter.61.cloned.1.call-update) | async-done | bytes 1179664 | tf_op jit(solution)/shard_map/reduce_scatter | solution.py:314
  1295.7 47.3 %reduce-scatter.73.cloned.1.call-done = bf16[768,768]{1,0:T(8,128)(2,1)} async-done(((bf16[3072,768]{1,0:T(8,128)(2,1)}), bf16[768,768]{1,0:T(8,128)(2,1)}) %reduce-scatter.73.cloned.1.call-update) | async-done | bytes 1179664 | tf_op jit(solution)/shard_map/reduce_scatter | solution.py:317
  1349.3 44.2 %reduce-scatter.69.cloned.1.call-done = bf16[768,768]{1,0:T(8,128)(2,1)} async-done(((bf16[3072,768]{1,0:T(8,128)(2,1)}), bf16[768,768]{1,0:T(8,128)(2,1)}) %reduce-scatter.69.cloned.1.call-update) | async-done | bytes 1179664 | tf_op jit(solution)/shard_map/reduce_scatter | solution.py:317
  1461.2 21.3 %reduce-scatter.81.cloned.1.call-done = bf16[192,6]{1,0:T(8,128)(2,1)} async-done(((bf16[768,6]{1,0:T(8,128)(2,1)}), bf16[192,6]{1,0:T(8,128)(2,1)}) %reduce-scatter.81.cloned.1.call-update) | async-done | bytes 2320
  1483.4 37.2 %all-reduce.10 = (f32[2,192]{1,0:T(2,128)S(1)}, f32[2,192]{1,0:T(2,128)S(1)}, f32[6,192]{1,0:T(8,128)S(1)}, f32[6,192]{1,0:T(8,128)S(1)}, f32[768]{0:T(1024)S(1)}, /*index=5*/f32[768]{0:T(1024)S(1)}) all-reduce(bf16[2,192]{1,0:T(2,128)(2,1)S(1)} %copy.226, ...), channel_id=43, replica_groups=mesh['clip'=8,'seq'=4] {'clip'}, use_global_device_ids=true, to_apply=%region_57.58.clone | all-reduce | flops 4608 | bytes 30720
  1522.8 25.8 %reduce-scatter.59.cloned.1.call-done = f32[24,768]{1,0:T(8,128)} async-done(((f32[192,768]{1,0:T(8,128)}), f32[24,768]{1,0:T(8,128)}) %reduce-scatter.59.cloned.1.call-update) | async-done | bytes 73744 | tf_op jit(solution)/shard_map/reduce_scatter | solution.py:332
  1548.6 65.3 %reduce-scatter.55.cloned.1.call-done = f32[24,768]{1,0:T(8,128)} async-done(((f32[192,768]{1,0:T(8,128)}), f32[24,768]{1,0:T(8,128)}) %reduce-scatter.55.cloned.1.call-update) | async-done | bytes 73744 | tf_op jit(solution)/shard_map/reduce_scatter | solution.py:332
  1615.5 66.9 %reduce-scatter.51.cloned.1.call-done = f32[24,2304]{1,0:T(8,128)} async-done(((f32[192,2304]{1,0:T(8,128)}), f32[24,2304]{1,0:T(8,128)}) %reduce-scatter.51.cloned.1.call-update) | async-done | bytes 221200 | tf_op jit(solution)/shard_map/reduce_scatter | solution.py:331
  1682.4 68.7 %reduce-scatter.47.cloned.1.call-done = f32[24,2304]{1,0:T(8,128)} async-done(((f32[192,2304]{1,0:T(8,128)}), f32[24,2304]{1,0:T(8,128)}) %reduce-scatter.47.cloned.1.call-update) | async-done | bytes 221200 | tf_op jit(solution)/shard_map/reduce_scatter | solution.py:331
  1753.0 69.4 %reduce-scatter.67.cloned.1.call-done = f32[24,3072]{1,0:T(8,128)} async-done(((f32[192,3072]{1,0:T(8,128)}), f32[24,3072]{1,0:T(8,128)}) %reduce-scatter.67.cloned.1.call-update) | async-done | bytes 294928 | tf_op jit(solution)/shard_map/reduce_scatter | solution.py:333
  1822.4 71.6 %reduce-scatter.63.cloned.1.call-done = f32[24,3072]{1,0:T(8,128)} async-done(((f32[192,3072]{1,0:T(8,128)}), f32[24,3072]{1,0:T(8,128)}) %reduce-scatter.63.cloned.1.call-update) | async-done | bytes 294928 | tf_op jit(solution)/shard_map/reduce_scatter | solution.py:333
  1895.9 69.7 %reduce-scatter.75.cloned.1.call-done = f32[96,768]{1,0:T(8,128)} async-done(((f32[768,768]{1,0:T(8,128)}), f32[96,768]{1,0:T(8,128)}) %reduce-scatter.75.cloned.1.call-update) | async-done | bytes 294928 | tf_op jit(solution)/shard_map/reduce_scatter | solution.py:334
  1965.7 71.6 %reduce-scatter.71.cloned.1.call-done = f32[96,768]{1,0:T(8,128)} async-done(((f32[768,768]{1,0:T(8,128)}), f32[96,768]{1,0:T(8,128)}) %reduce-scatter.71.cloned.1.call-update) | async-done | bytes 294928 | tf_op jit(solution)/shard_map/reduce_scatter | solution.py:334
  (716 shorter events, 676.9 us)
Async XLA Ops:
  7.2 158.7 %all-gather.31.cloned.1.call-start = ((), (), s32[]{:S(2)}) async-start(), calls=%async_computation.44 | async-start | bytes 3649536 | tf_op jit(solution)/shard_map/all_gather | solution.py:280
  8.9 253.5 %all-gather.33.cloned.1.call-start = ((), (), s32[]{:S(2)}) async-start(), calls=%async_computation.45 | async-start | bytes 1966080 | tf_op jit(solution)/shard_map/all_gather | solution.py:175
  171.4 153.4 %all-gather.37.cloned.1.call-start = ((), (), s32[]{:S(2)}) async-start(), calls=%async_computation.47 | async-start | bytes 1216512 | tf_op jit(solution)/shard_map/all_gather | solution.py:281
  172.1 160.2 %all-gather.39.cloned.1.call-start = ((), (), s32[]{:S(2)}) async-start(), calls=%async_computation.48 | async-start | bytes 4866048 | tf_op jit(solution)/shard_map/all_gather | solution.py:282
  172.9 225.2 %all-gather.41.cloned.1.call-start = ((), (), s32[]{:S(2)}) async-start(), calls=%async_computation.49 | async-start | bytes 4866048 | tf_op jit(solution)/shard_map/all_gather | solution.py:283
  173.7 286.3 %all-gather.43.cloned.1.call-start = ((), (), s32[]{:S(2)}) async-start(), calls=%async_computation.50 | async-start | bytes 3649536 | tf_op jit(solution)/shard_map/all_gather | solution.py:280
  174.5 308.5 %all-gather.45.cloned.1.call-start = ((), (), s32[]{:S(2)}) async-start(), calls=%async_computation.51 | async-start | bytes 1966080 | tf_op jit(solution)/shard_map/all_gather | solution.py:175
  465.2 98.1 %all-gather.49.cloned.1.call-start = ((), (), s32[]{:S(2)}) async-start(), calls=%async_computation.53 | async-start | bytes 1216512 | tf_op jit(solution)/shard_map/all_gather | solution.py:281
  465.8 162.3 %all-gather.51.cloned.1.call-start = ((), (), s32[]{:S(2)}) async-start(), calls=%async_computation.54 | async-start | bytes 4866048 | tf_op jit(solution)/shard_map/all_gather | solution.py:282
  466.5 226.8 %all-gather.53.cloned.1.call-start = ((), (), s32[]{:S(2)}) async-start(), calls=%async_computation.55 | async-start | bytes 4866048 | tf_op jit(solution)/shard_map/all_gather | solution.py:283
  467.1 375.3 %reduce-scatter.39.cloned.1.call-start = ((), (), s32[]{:S(2)}) async-start(), calls=%async_computation.25 | async-start | bytes 1966080 | tf_op jit(solution)/shard_map/reduce_scatter | solution.py:233
  815.8 202.5 %reduce-scatter.43.cloned.1.call-start = ((), (), s32[]{:S(2)}) async-start(), calls=%async_computation.27 | async-start | bytes 1966080 | tf_op jit(solution)/shard_map/reduce_scatter | solution.py:233
  991.7 108.3 %reduce-scatter.57.cloned.1.call-start = ((), (), s32[]{:S(2)}) async-start(), calls=%async_computation.34 | async-start | bytes 1474560 | tf_op jit(solution)/shard_map/reduce_scatter | solution.py:311
  994.5 111.0 %reduce-scatter.53.cloned.1.call-start = ((), (), s32[]{:S(2)}) async-start(), calls=%async_computation.32 | async-start | bytes 1474560 | tf_op jit(solution)/shard_map/reduce_scatter | solution.py:311
  996.2 152.4 %reduce-scatter.49.cloned.1.call-start = ((), (), s32[]{:S(2)}) async-start(), calls=%async_computation.30 | async-start | bytes 4423680 | tf_op jit(solution)/shard_map/reduce_scatter | solution.py:308
  1001.0 190.6 %reduce-scatter.45.cloned.1.call-start = ((), (), s32[]{:S(2)}) async-start(), calls=%async_computation.28 | async-start | bytes 4423680 | tf_op jit(solution)/shard_map/reduce_scatter | solution.py:308
  1058.1 183.9 %reduce-scatter.65.cloned.1.call-start = ((), (), s32[]{:S(2)}) async-start(), calls=%async_computation.38 | async-start | bytes 5898240 | tf_op jit(solution)/shard_map/reduce_scatter | solution.py:314
  1064.7 227.9 %reduce-scatter.61.cloned.1.call-start = ((), (), s32[]{:S(2)}) async-start(), calls=%async_computation.36 | async-start | bytes 5898240 | tf_op jit(solution)/shard_map/reduce_scatter | solution.py:314
  1071.4 271.7 %reduce-scatter.73.cloned.1.call-start = ((), (), s32[]{:S(2)}) async-start(), calls=%async_computation.42 | async-start | bytes 5898240 | tf_op jit(solution)/shard_map/reduce_scatter | solution.py:317
  1078.2 315.3 %reduce-scatter.69.cloned.1.call-start = ((), (), s32[]{:S(2)}) async-start(), calls=%async_computation.40 | async-start | bytes 5898240 | tf_op jit(solution)/shard_map/reduce_scatter | solution.py:317
  1084.7 333.9 %reduce-scatter.79.cloned.1.call-start = ((), (), s32[]{:S(2)}) async-start(), calls=%async_computation.57 | async-start | bytes 245760
  1091.7 346.6 %reduce-scatter.83.cloned.1.call-start = ((), (), s32[]{:S(2)}) async-start(), calls=%async_computation.59 | async-start | bytes 245760
  1095.9 364.5 %reduce-scatter.77.cloned.1.call-start = ((), (), s32[]{:S(2)}) async-start(), calls=%async_computation.56 | async-start | bytes 245760
  1098.9 383.7 %reduce-scatter.81.cloned.1.call-start = ((), (), s32[]{:S(2)}) async-start(), calls=%async_computation.58 | async-start | bytes 245760
  1100.0 448.6 %reduce-scatter.59.cloned.1.call-start = ((), (), s32[]{:S(2)}) async-start(), calls=%async_computation.35 | async-start | bytes 663552 | tf_op jit(solution)/shard_map/reduce_scatter | solution.py:332
  1101.9 512.0 %reduce-scatter.55.cloned.1.call-start = ((), (), s32[]{:S(2)}) async-start(), calls=%async_computation.33 | async-start | bytes 663552 | tf_op jit(solution)/shard_map/reduce_scatter | solution.py:332
  1107.4 575.0 %reduce-scatter.51.cloned.1.call-start = ((), (), s32[]{:S(2)}) async-start(), calls=%async_computation.31 | async-start | bytes 1990656 | tf_op jit(solution)/shard_map/reduce_scatter | solution.py:331
  1151.1 600.0 %reduce-scatter.47.cloned.1.call-start = ((), (), s32[]{:S(2)}) async-start(), calls=%async_computation.29 | async-start | bytes 1990656 | tf_op jit(solution)/shard_map/reduce_scatter | solution.py:331
  1194.2 628.2 %reduce-scatter.67.cloned.1.call-start = ((), (), s32[]{:S(2)}) async-start(), calls=%async_computation.39 | async-start | bytes 2654208 | tf_op jit(solution)/shard_map/reduce_scatter | solution.py:333
  1245.0 649.0 %reduce-scatter.63.cloned.1.call-start = ((), (), s32[]{:S(2)}) async-start(), calls=%async_computation.37 | async-start | bytes 2654208 | tf_op jit(solution)/shard_map/reduce_scatter | solution.py:333
  1295.7 670.0 %reduce-scatter.75.cloned.1.call-start = ((), (), s32[]{:S(2)}) async-start(), calls=%async_computation.43 | async-start | bytes 2654208 | tf_op jit(solution)/shard_map/reduce_scatter | solution.py:334
  1345.9 691.3 %reduce-scatter.71.cloned.1.call-start = ((), (), s32[]{:S(2)}) async-start(), calls=%async_computation.41 | async-start | bytes 2654208 | tf_op jit(solution)/shard_map/reduce_scatter | solution.py:334
  (79 other events, 1075.1 us)
Sparse Core Ops, SparseCore 0:
  11.5 63.4 all-gather.30
  212.3 54.1 all-gather.36
  269.8 62.4 all-gather.38
  335.6 62.4 all-gather.40
  401.0 58.9 all-gather.42
  507.6 54.3 all-gather.48
  565.5 62.4 all-gather.50
  630.8 62.4 all-gather.52
  815.3 26.9 reduce-scatter.38
  844.9 28.1 reduce-scatter.36
  990.1 28.1 reduce-scatter.42
  1020.9 28.1 reduce-scatter.40
  1051.5 25.7 reduce-scatter.56
  1079.8 25.7 reduce-scatter.52
  1108.1 40.4 reduce-scatter.48
  1151.2 40.4 reduce-scatter.44
  1194.2 47.8 reduce-scatter.64
  1244.7 47.8 reduce-scatter.60
  1295.2 47.8 reduce-scatter.72
  1345.6 47.8 reduce-scatter.68
  1396.5 19.7 reduce-scatter.78
  1418.6 19.7 reduce-scatter.82
  1440.6 19.7 reduce-scatter.76
  1462.8 19.7 reduce-scatter.80
  1486.4 62.1 reduce-scatter.58
  1552.7 61.1 reduce-scatter.54
  1617.4 64.9 reduce-scatter.50
  1686.3 64.8 reduce-scatter.46
  1754.5 67.8 reduce-scatter.66
  1825.9 68.0 reduce-scatter.62
  1897.5 68.0 reduce-scatter.74
  1969.0 68.1 reduce-scatter.70
  (4 shorter events, 74.4 us)
where the time goes:
time: 2060 us; the launch traced here: 2050 us
  waiting for transfers between devices  1200 us (58%)
  matrix products  347 us (17%)
  blocking collectives  249 us (12%)
  local copies, waits for them, and re-layouts  171 us (8%)
  other arithmetic  55 us (3%)
    reduce_scatter x2, waiting for transfers between devices, body(): lax.psum_scatter(halves[3], 'clip', scatter_dimension=0, tiled=True)  141 us
    reduce_scatter x2, waiting for transfers between devices, body(): lax.psum_scatter(halves[2], 'clip', scatter_dimension=0, tiled=True)  141 us
    reduce_scatter x2, waiting for transfers between devices, body(): lax.psum_scatter(halves[0], 'clip', scatter_dimension=0, tiled=True)  136 us
    all_gather x2, waiting for transfers between devices, body(): lax.all_gather(mlp_out[layer_index], ('clip', 'seq'), axis=0, tiled=True)  108 us
    reduce_scatter x2, waiting for transfers between devices, body(): lax.psum_scatter(ordered[2].astype(jnp.bfloat16), 'seq', scatter_dimensio...  95.3 us
    reduce_scatter x2, waiting for transfers between devices, body(): lax.psum_scatter(ordered[3].astype(jnp.bfloat16), 'seq', scatter_dimensio...  91.5 us
    reduce_scatter x2, waiting for transfers between devices, body(): lax.psum_scatter(halves[1], 'clip', scatter_dimension=0, tiled=True)  91.1 us
    unnamed x3, blocking collectives  84.6 us
  transfers between devices with their start and end apart: 36, of which 29 were waited for; matrix products, arithmetic and copies ran while one was open for 15% of the time, Pallas kernels for 0%

commit v1 on v0

v1 whole, which is shorter than its diff:
```python
import functools

import jax
import jax.numpy as jnp
from jax import lax
from jax.experimental import pallas as pl
from jax.experimental.pallas import tpu as pltpu
from jax.sharding import PartitionSpec as P

D = 768
H = 12
HD = 64


eps_norm = 1e-05
root_half = 0.7071067811865476
inv_root_two_pi = 0.3989422804014327


def product(left, right):
    return jnp.dot(left, right, preferred_element_type=jnp.float32)


def product_left(left, right):
    return lax.dot_general(
        left, right, (((0,), (0,)), ((), ())), preferred_element_type=jnp.float32
    )


def product_right(left, right):
    return lax.dot_general(
        left, right, (((1,), (1,)), ((), ())), preferred_element_type=jnp.float32
    )


def norm_forward(rows, gain, shift):
    center = rows - jnp.mean(rows, axis=1, keepdims=True)
    inv_scale = lax.rsqrt(jnp.mean(center * center, axis=1, keepdims=True) + eps_norm)
    unit_rows = center * inv_scale
    return (unit_rows * gain + shift, unit_rows, inv_scale)


def norm_backward(upstream, unit_rows, inv_scale, gain):
    scaled = upstream * gain
    mean_plain = jnp.mean(scaled, axis=1, keepdims=True)
    mean_unit = jnp.mean(scaled * unit_rows, axis=1, keepdims=True)
    back = inv_scale * (scaled - mean_plain - unit_rows * mean_unit)
    return (back, jnp.sum(upstream * unit_rows, axis=0), jnp.sum(upstream, axis=0))


def gelu_slope(pre_gelu):
    cumulative = 0.5 * (1.0 + lax.erf(pre_gelu * root_half))
    density = jnp.exp(-0.5 * pre_gelu * pre_gelu) * inv_root_two_pi
    return cumulative + pre_gelu * density


def column_sums(rows):
    return jnp.sum(rows.astype(jnp.float32), axis=0)


def bit_of(index, weight):
    return lax.rem(lax.div(index, weight), 2)


def flip(index, weight):
    return index + weight - 2 * weight * bit_of(index, weight)


def bit_orders(clip_size, seq_size, with_clip=True):
    high = []
    weight = clip_size * seq_size // 2
    while weight >= seq_size and with_clip:
        high.append(weight)
        weight //= 2
    low = []
    weight = seq_size // 2
    while weight >= 1:
        low.append(weight)
        weight //= 2
    first = high + low
    if not high:
        return (first, first)
    second = high[:-1] + [low[0], high[-1]] + low[1:]
    return (first, second)


def spread(position, weights):
    total = 0
    for place, weight in enumerate(weights):
        total = total + weight * lax.rem(lax.div(position, 2**place), 2)
    return total


def partner_id(weight, seq_size):
    clip_at, seq_at = lax.axis_index("clip"), lax.axis_index("seq")
    if weight < seq_size:
        return {"clip": clip_at, "seq": flip(seq_at, weight)}
    return {"clip": flip(clip_at, weight // seq_size), "seq": seq_at}


def greet(weights, seq_size):
    barrier = pltpu.get_barrier_semaphore()
    for weight in weights:
        pl.semaphore_signal(
            barrier,
            inc=1,
            device_id=partner_id(weight, seq_size),
            device_id_type=pl.DeviceIdType.MESH,
        )
    pl.semaphore_wait(barrier, len(weights))


def round_up(value, step):
    return (value + step - 1) // step * step


def halves_of(rows):
    first = round_up(rows // 2, 16)
    if first >= rows:
        return ((0, rows),)
    return ((0, first), (first, rows - first))


def cube_gather(shard, clip_size, seq_size, with_clip, collective_id):
    parts, rows, columns = shard.shape
    count = clip_size * seq_size if with_clip else seq_size
    orders = bit_orders(clip_size, seq_size, with_clip)
    chains = [
        (part, start, size, orders[place % 2])
        for part in range(parts)
        for place, (start, size) in enumerate(halves_of(rows))
    ]
    stages = len(orders[0])

    def kernel(in_ref, out_ref, own_sem, send_sem, recv_sem):
        greet(orders[0], seq_size)
        me = lax.axis_index("seq")
        if with_clip:
            me = lax.axis_index("clip") * seq_size + me
        own = []
        for part in range(parts):
            copy = pltpu.make_async_copy(in_ref.at[part], out_ref.at[part, me], own_sem.at[part])
            copy.start()
            own.append(copy)
        for copy in own:
            copy.wait()

        def start_stage(chain_at, stage):
            part, start, size, order = chains[chain_at]
            weight = order[stage]
            base = me
            for done in order[:stage]:
                base = base - done * bit_of(me, done)

            def one(position, carry):
                place = base + spread(position, order[:stage])
                block = out_ref.at[part, place, pl.ds(start, size)]
                pltpu.make_async_remote_copy(
                    src_ref=block,
                    dst_ref=block,
                    send_sem=send_sem.at[chain_at, stage],
                    recv_sem=recv_sem.at[chain_at, stage],
                    device_id=partner_id(weight, seq_size),
                    device_id_type=pl.DeviceIdType.MESH,
                ).start()
                return carry

            if stage == 0:
                one(0, 0)
            else:
                lax.fori_loop(0, 2**stage, one, 0)

        def wait_stage(chain_at, stage):
            part, start, size, order = chains[chain_at]
            block = out_ref.at[part, pl.ds(0, 2**stage), pl.ds(start, size)]
            pltpu.make_async_remote_copy(
                src_ref=block,
                dst_ref=block,
                send_sem=send_sem.at[chain_at, stage],
                recv_sem=recv_sem.at[chain_at, stage],
                device_id=partner_id(order[stage], seq_size),
                device_id_type=pl.DeviceIdType.MESH,
            ).wait()

        for tick in range(stages + parts):
            for chain_at, chain in enumerate(chains):
                stage = tick - chain[0]
                if 1 <= stage <= stages:
                    wait_stage(chain_at, stage - 1)
                if 0 <= stage < stages:
                    start_stage(chain_at, stage)

    return pl.pallas_call(
        kernel,
        out_shape=jax.ShapeDtypeStruct((parts, count, rows, columns), shard.dtype),
        in_specs=[pl.BlockSpec(memory_space=pl.ANY)],
        out_specs=pl.BlockSpec(memory_space=pl.ANY),
        scratch_shapes=[
            pltpu.SemaphoreType.DMA((parts,)),
            pltpu.SemaphoreType.DMA((len(chains), stages)),
            pltpu.SemaphoreType.DMA((len(chains), stages)),
        ],
        compiler_params=pltpu.CompilerParams(
            collective_id=collective_id, has_side_effects=True, vmem_limit_bytes=16 * 2**20
        ),
    )(shard)


def cube_scatter(terms, clip_size, seq_size, with_clip, collective_id, out_dtype=jnp.float32):
    count, rows, columns = terms.shape
    orders = [order[::-1] for order in bit_orders(clip_size, seq_size, with_clip)]
    chains = [
        (start, size, orders[place % 2]) for place, (start, size) in enumerate(halves_of(rows))
    ]
    stages = len(orders[0])
    offsets = [sum(count // 2 ** (s + 1) for s in range(stage)) for stage in range(stages)]

    def kernel(in_ref, out_ref, total, landed, own_sem, send_sem, recv_sem):
        greet(orders[0], seq_size)
        me = lax.axis_index("seq")
        if with_clip:
            me = lax.axis_index("clip") * seq_size + me

        def places(chain_at, stage):
            order = chains[chain_at][2]
            base = me
            for later in order[stage:]:
                base = base - later * bit_of(me, later)
            weight = order[stage]
            mine = base + weight * bit_of(me, weight)
            theirs = base + weight - weight * bit_of(me, weight)
            return mine, theirs, order[stage + 1 :], weight

        def start_stage(chain_at, stage):
            start, size, order = chains[chain_at]
            mine, theirs, rest, weight = places(chain_at, stage)
            source = in_ref if stage == 0 else total

            def one(position, carry):
                pltpu.make_async_remote_copy(
                    src_ref=source.at[theirs + spread(position, rest), pl.ds(start, size)],
                    dst_ref=landed.at[offsets[stage] + position, pl.ds(start, size)],
                    send_sem=send_sem.at[chain_at, stage],
                    recv_sem=recv_sem.at[chain_at, stage],
                    device_id=partner_id(weight, seq_size),
                    device_id_type=pl.DeviceIdType.MESH,
                ).start()
                return carry

            if stage == stages - 1:
                one(0, 0)
            else:
                lax.fori_loop(0, 2 ** (stages - 1 - stage), one, 0)

        def load_own(chain_at):
            start, size, order = chains[chain_at]
            mine, theirs, rest, weight = places(chain_at, 0)

            def one(position, carry):
                place = mine + spread(position, rest)
                pltpu.make_async_copy(
                    in_ref.at[place, pl.ds(start, size)],
                    total.at[place, pl.ds(start, size)],
                    own_sem.at[chain_at],
                ).start()
                return carry

            lax.fori_loop(0, count // 2, one, 0)

        def wait_own(chain_at):
            start, size, order = chains[chain_at]
            block = pl.ds(0, count // 2), pl.ds(start, size)
            pltpu.make_async_copy(in_ref.at[block], total.at[block], own_sem.at[chain_at]).wait()

        def finish_stage(chain_at, stage):
            start, size, order = chains[chain_at]
            mine, theirs, rest, weight = places(chain_at, stage)
            blocks = 2 ** (stages - 1 - stage)
            source = in_ref if stage == 0 else total
            pltpu.make_async_remote_copy(
                src_ref=source.at[pl.ds(0, blocks), pl.ds(start, size)],
                dst_ref=landed.at[pl.ds(offsets[stage], blocks), pl.ds(start, size)],
                send_sem=send_sem.at[chain_at, stage],
                recv_sem=recv_sem.at[chain_at, stage],
                device_id=partner_id(weight, seq_size),
                device_id_type=pl.DeviceIdType.MESH,
            ).wait()
            if stage == 0:
                wait_own(chain_at)
            tiles = size // 16

            def add(step, carry):
                position, tile = lax.div(step, tiles), lax.rem(step, tiles)
                place = mine + spread(position, rest)
                row = pl.ds(pl.multiple_of(start + tile * 16, 16), 16)
                summed = total[place, row, :].astype(jnp.float32) + landed[
                    offsets[stage] + position, row, :
                ].astype(jnp.float32)
                if stage == stages - 1:
                    out_ref[row, :] = summed.astype(out_ref.dtype)
                else:
                    total[place, row, :] = summed.astype(jnp.bfloat16)
                return carry

            lax.fori_loop(0, blocks * tiles, add, 0)

        for chain_at in range(len(chains)):
            start_stage(chain_at, 0)
        for chain_at in range(len(chains)):
            load_own(chain_at)
        for stage in range(stages):
            for chain_at in range(len(chains)):
                finish_stage(chain_at, stage)
                if stage + 1 < stages:
                    start_stage(chain_at, stage + 1)

    return pl.pallas_call(
        kernel,
        out_shape=jax.ShapeDtypeStruct((rows, columns), out_dtype),
        in_specs=[pl.BlockSpec(memory_space=pl.ANY)],
        out_specs=pl.BlockSpec(memory_space=pltpu.VMEM),
        scratch_shapes=[
            pltpu.VMEM((count, rows, columns), terms.dtype),
            pltpu.VMEM((count - 1, rows, columns), terms.dtype),
            pltpu.SemaphoreType.DMA((len(chains),)),
            pltpu.SemaphoreType.DMA((len(chains), stages)),
            pltpu.SemaphoreType.DMA((len(chains), stages)),
        ],
        compiler_params=pltpu.CompilerParams(
            collective_id=collective_id, has_side_effects=True, vmem_limit_bytes=48 * 2**20
        ),
    )(terms)


def head_pair(ref, head):
    return ref[:, head * HD : (head + 1) * HD]


def probabilities(query, key):
    scores = product_right(query, key) * (HD ** (-0.5))
    powers = jnp.exp(scores - jnp.max(scores, axis=1, keepdims=True))
    return powers * (1.0 / jnp.sum(powers, axis=1, keepdims=True))


def attend_forward_kernel(q_ref, k_ref, v_ref, o_ref):
    outputs = []
    for head in range(2):
        probs = probabilities(head_pair(q_ref, head), head_pair(k_ref, head))
        outputs.append(product(probs.astype(jnp.bfloat16), head_pair(v_ref, head)))
    o_ref[...] = jnp.concatenate(outputs, axis=1).astype(o_ref.dtype)


def attend_backward_kernel(q_ref, k_ref, v_ref, go_ref, gq_ref, gk_ref, gv_ref):
    grads = ([], [], [])
    for head in range(2):
        query, key = head_pair(q_ref, head), head_pair(k_ref, head)
        value, upstream = head_pair(v_ref, head), head_pair(go_ref, head)
        probs = probabilities(query, key)
        grad_probs = product_right(upstream, value)
        inner = jnp.sum(grad_probs * probs, axis=1, keepdims=True)
        grad_scores = (probs * (grad_probs - inner)).astype(jnp.bfloat16)
        grads[0].append(product(grad_scores, key) * (HD ** (-0.5)))
        grads[1].append(product_left(grad_scores, query) * (HD ** (-0.5)))
        grads[2].append(product_left(probs.astype(jnp.bfloat16), upstream))
    for ref, pieces in zip((gq_ref, gk_ref, gv_ref), grads):
        ref[...] = jnp.concatenate(pieces, axis=1).astype(ref.dtype)


def attend_forward(projected, key_values):
    rows, length = projected.shape[0], key_values.shape[0]
    pairs = D // (2 * HD)
    return pl.pallas_call(
        attend_forward_kernel,
        grid=(pairs,),
        out_shape=jax.ShapeDtypeStruct((rows, D), jnp.bfloat16),
        in_specs=[
            pl.BlockSpec((rows, 2 * HD), lambda pair: (0, pair)),
            pl.BlockSpec((length, 2 * HD), lambda pair: (0, pair)),
            pl.BlockSpec((length, 2 * HD), lambda pair: (0, pair + pairs)),
        ],
        out_specs=pl.BlockSpec((rows, 2 * HD), lambda pair: (0, pair)),
        compiler_params=pltpu.CompilerParams(vmem_limit_bytes=40 * 2**20),
    )(projected, key_values, key_values)


def attend_backward(projected, key_values, grad_attended):
    rows, length = projected.shape[0], key_values.shape[0]
    pairs = D // (2 * HD)
    return pl.pallas_call(
        attend_backward_kernel,
        grid=(pairs,),
        out_shape=(
            jax.ShapeDtypeStruct((rows, D), jnp.bfloat16),
            jax.ShapeDtypeStruct((length, D), jnp.bfloat16),
            jax.ShapeDtypeStruct((length, D), jnp.bfloat16),
        ),
        in_specs=[
            pl.BlockSpec((rows, 2 * HD), lambda pair: (0, pair)),
            pl.BlockSpec((length, 2 * HD), lambda pair: (0, pair)),
            pl.BlockSpec((length, 2 * HD), lambda pair: (0, pair + pairs)),
            pl.BlockSpec((rows, 2 * HD), lambda pair: (0, pair)),
        ],
        out_specs=(
            pl.BlockSpec((rows, 2 * HD), lambda pair: (0, pair)),
            pl.BlockSpec((length, 2 * HD), lambda pair: (0, pair)),
            pl.BlockSpec((length, 2 * HD), lambda pair: (0, pair)),
        ),
        compiler_params=pltpu.CompilerParams(vmem_limit_bytes=48 * 2**20),
    )(projected, key_values, key_values, grad_attended)


def pack_shards(attn_in, attn_out, mlp_in, mlp_out, norm_gains, shifts, mlp_bias):
    layers, depth = attn_in.shape[0], attn_in.shape[1]
    small = jnp.concatenate(
        [norm_gains.reshape(layers, -1), shifts.reshape(layers, -1), mlp_bias], axis=1
    )
    small_rows = (small.shape[1] + D - 1) // D
    small = jnp.pad(small, ((0, 0), (0, small_rows * D - small.shape[1])))
    small = small.reshape(layers, small_rows, D)
    blocks = [attn_in[:, :, at : at + D] for at in range(0, attn_in.shape[2], D)]
    blocks.append(attn_out)
    blocks += [mlp_in[:, :, at : at + D] for at in range(0, mlp_in.shape[2], D)]
    blocks += [mlp_out, small]
    rows = sum(block.shape[1] for block in blocks)
    padding = round_up(rows, 16) - rows
    blocks.append(jnp.zeros((layers, padding, D), attn_in.dtype))
    return jnp.concatenate(blocks, axis=1)


def columns_back(gathered, first, blocks, depth):
    count = gathered.shape[0]
    piece = gathered[:, first : first + blocks * depth].reshape(count, blocks, depth, D)
    return piece.transpose(0, 2, 1, 3).reshape(count * depth, blocks * D)


def unpack_layer(gathered, depth):
    count = gathered.shape[0]
    w_attn_in = columns_back(gathered, 0, 3, depth)
    w_attn_out = columns_back(gathered, 3 * depth, 1, depth)
    w_mlp_in = columns_back(gathered, 4 * depth, 4, depth)
    w_mlp_out = gathered[:, 8 * depth : 12 * depth].reshape(4 * count * depth, D)
    small_rows = (12 * depth + D - 1) // D
    small = gathered[:, 12 * depth : 12 * depth + small_rows].reshape(count, -1)
    small = small.astype(jnp.float32)
    gains = small[:, : 2 * depth].reshape(count, 2, depth).transpose(1, 0, 2).reshape(2, D)
    shift_rows = small[:, 2 * depth : 8 * depth].reshape(count, 6, depth)
    shift_rows = shift_rows.transpose(1, 0, 2).reshape(6, D)
    bias_mlp = small[:, 8 * depth : 12 * depth].reshape(4 * D)
    return (w_attn_in, w_attn_out, w_mlp_in, w_mlp_out, gains, shift_rows, bias_mlp)


def columns_apart(term, count):
    depth, blocks = term.shape[0] // count, term.shape[1] // D
    term = term.astype(jnp.bfloat16).reshape(count, depth, blocks, D)
    return term.transpose(0, 2, 1, 3).reshape(count, blocks * depth, D)


def pack_grads(grad_terms, count, rows):
    grad_attn_in, grad_attn_out, grad_mlp_in, grad_mlp_out, gains, shift_rows, bias = grad_terms
    depth = D // count
    small = jnp.concatenate(
        [
            gains.reshape(2, count, depth).transpose(1, 0, 2).reshape(count, -1),
            shift_rows.reshape(6, count, depth).transpose(1, 0, 2).reshape(count, -1),
            bias.reshape(count, -1),
        ],
        axis=1,
    ).astype(jnp.bfloat16)
    small_rows = (small.shape[1] + D - 1) // D
    small = jnp.pad(small, ((0, 0), (0, small_rows * D - small.shape[1])))
    blocks = [
        columns_apart(grad_attn_in, count),
        columns_apart(grad_attn_out, count),
        columns_apart(grad_mlp_in, count),
        grad_mlp_out.astype(jnp.bfloat16).reshape(count, 4 * depth, D),
        small.reshape(count, small_rows, D),
    ]
    padding = rows - sum(block.shape[1] for block in blocks)
    blocks.append(jnp.zeros((count, padding, D), jnp.bfloat16))
    return jnp.concatenate(blocks, axis=1)


def unpack_shard(summed, depth):
    def across(first, blocks):
        return jnp.concatenate(
            [summed[first + at * depth : first + (at + 1) * depth] for at in range(blocks)], axis=1
        )

    small_rows = (12 * depth + D - 1) // D
    small = summed[12 * depth : 12 * depth + small_rows].reshape(-1)
    return (
        across(0, 3),
        across(3 * depth, 1),
        across(4 * depth, 4),
        summed[8 * depth : 12 * depth],
        small[: 2 * depth].reshape(2, depth),
        small[2 * depth : 8 * depth].reshape(6, depth),
        small[8 * depth : 12 * depth],
    )


def layer_forward(residual, weights, sizes, layer_index):
    w_attn_in, w_attn_out, w_mlp_in, w_mlp_out, gain_rows, shift_rows, bias_mlp = weights
    normed = norm_forward(residual, gain_rows[0], shift_rows[0])[0].astype(jnp.bfloat16)
    qkv_bias = jnp.concatenate([shift_rows[1], jnp.zeros_like(shift_rows[1]), shift_rows[2]])
    projected = (product(normed, w_attn_in) + qkv_bias).astype(jnp.bfloat16)
    key_values = cube_gather(projected[None, :, D:], *sizes, False, 2 + layer_index)
    key_values = key_values.reshape(-1, 2 * D)
    attended = attend_forward(projected, key_values)
    middle = residual + product(attended, w_attn_out) + shift_rows[3]
    normed_two = norm_forward(middle, gain_rows[1], shift_rows[4])[0].astype(jnp.bfloat16)
    pre_gelu = product(normed_two, w_mlp_in) + bias_mlp
    hidden = jax.nn.gelu(pre_gelu, approximate=False).astype(jnp.bfloat16)
    result = middle + product(hidden, w_mlp_out) + shift_rows[5]
    saved = (residual, normed, projected, key_values, attended, middle, normed_two, pre_gelu, hidden)
    return (result, saved)


def layer_backward(upstream, saved, weights, sizes, layer_index):
    w_attn_in, w_attn_out, w_mlp_in, w_mlp_out, gain_rows, shift_rows, bias_mlp = weights
    residual, normed, projected, key_values, attended, middle, normed_two, pre_gelu, hidden = saved
    upstream_low = upstream.astype(jnp.bfloat16)
    grad_mlp_out = product_left(hidden, upstream_low)
    grad_bias_two = column_sums(upstream_low)
    grad_pre = (product_right(upstream_low, w_mlp_out) * gelu_slope(pre_gelu)).astype(jnp.bfloat16)
    grad_mlp_in = product_left(normed_two, grad_pre)
    grad_mlp_bias = column_sums(grad_pre)
    grad_normed_two = product_right(grad_pre, w_mlp_in)
    unit_two, scale_two = norm_forward(middle, gain_rows[1], shift_rows[4])[1:]
    back_two, grad_gain_two, grad_shift_two = norm_backward(
        grad_normed_two, unit_two, scale_two, gain_rows[1]
    )
    grad_middle = upstream + back_two
    middle_low = grad_middle.astype(jnp.bfloat16)
    grad_attn_out = product_left(attended, middle_low)
    grad_bias_out = column_sums(middle_low)
    grad_attended = product_right(middle_low, w_attn_out).astype(jnp.bfloat16)
    grad_queries, key_terms, value_terms = attend_backward(projected, key_values, grad_attended)
    rows = grad_queries.shape[0]
    terms = jnp.concatenate([key_terms, value_terms], axis=1).reshape(-1, rows, 2 * D)
    grad_key_values = cube_scatter(terms, *sizes, False, 4 + layer_index, jnp.bfloat16)
    grad_projected = jnp.concatenate([grad_queries, grad_key_values], axis=1)
    grad_attn_in = product_left(normed, grad_projected)
    projected_sums = column_sums(grad_projected)
    grad_normed = product_right(grad_projected, w_attn_in)
    unit_one, scale_one = norm_forward(residual, gain_rows[0], shift_rows[0])[1:]
    back_one, grad_gain_one, grad_shift_one = norm_backward(
        grad_normed, unit_one, scale_one, gain_rows[0]
    )
    grad_residual = grad_middle + back_one
    grad_gains = jnp.stack([grad_gain_one, grad_gain_two])
    grad_shifts = jnp.stack(
        [
            grad_shift_one,
            projected_sums[:D],
            projected_sums[2 * D :],
            grad_bias_out,
            grad_shift_two,
            grad_bias_two,
        ]
    )
    grad_terms = (
        grad_attn_in,
        grad_attn_out,
        grad_mlp_in,
        grad_mlp_out,
        grad_gains,
        grad_shifts,
        grad_mlp_bias,
    )
    return (grad_residual, grad_terms)


def body(sizes, frames, out_grad, *params):
    layers, depth = params[0].shape[0], params[0].shape[1]
    count = sizes[0] * sizes[1]
    groups, frame_count, width = frames.shape
    residual = frames.astype(jnp.float32).reshape(groups * frame_count, width)
    packed = pack_shards(*params)
    gathered = cube_gather(packed, *sizes, True, 1)
    weights = [unpack_layer(gathered[layer], depth) for layer in range(layers)]
    saved_all = []
    for layer in range(layers):
        residual, saved = layer_forward(residual, weights[layer], sizes, layer)
        saved_all.append(saved)
    encoded = residual.astype(jnp.bfloat16).reshape(groups, frame_count, width)
    upstream = out_grad.astype(jnp.float32).reshape(groups * frame_count, width)
    shards = [None] * layers
    for layer in reversed(range(layers)):
        upstream, grad_terms = layer_backward(
            upstream, saved_all[layer], weights[layer], sizes, layer
        )
        terms = pack_grads(grad_terms, count, packed.shape[1])
        shards[layer] = unpack_shard(cube_scatter(terms, *sizes, True, 6 + layer), depth)
    outputs = tuple(jnp.stack(pieces) for pieces in zip(*shards))
    return (encoded, upstream.reshape(groups, frame_count, width)) + outputs


def solution(mesh):
    sizes = (mesh.shape["clip"], mesh.shape["seq"])
    specs = (
        P("clip", "seq", None),
        P("clip", "seq", None),
        P(None, ("clip", "seq"), None),
        P(None, ("clip", "seq"), None),
        P(None, ("clip", "seq"), None),
        P(None, ("clip", "seq"), None),
        P(None, None, ("clip", "seq")),
        P(None, None, ("clip", "seq")),
        P(None, ("clip", "seq")),
    )
    return jax.shard_map(
        functools.partial(body, sizes), mesh=mesh, in_specs=specs, out_specs=specs, check_vma=False
    )
```

time: 2060 us -> 962 us (0.47)
  waiting for transfers between devices: 1200 us -> 0 us
  Pallas kernels: 0 us -> 574 us
  matrix products: 347 us -> 83.1 us
  blocking collectives: 249 us -> 0 us
  local copies, waits for them, and re-layouts: 171 us -> 274 us
  other arithmetic: 55 us -> 13.3 us
    reduce_scatter x20 -> x0, waiting for transfers between devices: 885 us -> none  [the longest x2 141 us: body(): lax.psum_scatter(halves[3], 'clip', scatter_dimension=0, tiled=True)]
    pallas_call x0 -> x11, Pallas kernels: none -> 574 us  [the longest x4 284 us: cube_scatter(): pl.pallas_call(kernel, out_shape=jax.ShapeDtypeStruct((rows, columns), ou...]
    dot_general x168 -> x0, matrix products: 254 us -> none  [the longest x48 60.8 us: one_head(): jnp.einsum('gqd,gkd->gqk', query_head, key_head, preferred_element_type=j...]
    all_gather x12 -> x0, waiting for transfers between devices: 254 us -> none  [the longest x2 108 us: body(): lax.all_gather(mlp_out[layer_index], ('clip', 'seq'), axis=0, tiled=True)]
    all_gather x4 -> x0, blocking collectives: 164 us -> none  [the longest x2 83.1 us: body(): lax.all_gather(shifts[layer_index], ('clip', 'seq'), axis=1, tiled=True)]
    concatenate x0 -> x3, local copies, waits for them, and re-layouts: none -> 148 us  [the longest x2 145 us: pack_grads(): return jnp.concatenate(blocks, axis=1)]
    unnamed x3 -> x0, blocking collectives: 84.6 us -> none
    unnamed x40 -> x0, waiting for transfers between devices: 64.9 us -> none
  transfers between devices with their start and end apart: 36 -> 0, of which waited for: 29 -> 0; matrix products, arithmetic and copies ran while one was open for 15% -> 0% of each run, Pallas kernels for 0% -> 0%
where the time goes in v1:
time: 962 us; the launch traced here: 947 us
  Pallas kernels  574 us (60%)
  local copies, waits for them, and re-layouts  274 us (28%)
  matrix products  83.1 us (9%)
  other arithmetic  13.3 us (1%)
    pallas_call x4, Pallas kernels, cube_scatter(): pl.pallas_call(kernel, out_shape=jax.ShapeDtypeStruct((rows, columns), ou...  284 us
    pallas_call x3, Pallas kernels, cube_gather(): pl.pallas_call(kernel, out_shape=jax.ShapeDtypeStruct((parts, count, rows...  237 us
    concatenate x2, local copies, waits for them, and re-layouts, pack_grads(): return jnp.concatenate(blocks, axis=1)  145 us
    reshape x6, local copies, waits for them, and re-layouts, columns_apart(): term = term.astype(jnp.bfloat16).reshape(count, depth, blocks, D)  48.5 us
    dot_general x8, matrix products, product(): return jnp.dot(left, right, preferred_element_type=jnp.float32)  39.1 us
    pallas_call x2, Pallas kernels, attend_backward(): pl.pallas_call(attend_backward_kernel, grid=(pairs,), out_shape=(jax.Shap...  33 us
    dot_general x8, matrix products, product_left(): lax.dot_general(left, right, (((0,), (0,)), ((), ())), preferred_element_...  23.9 us
    pallas_call x2, Pallas kernels, attend_forward(): pl.pallas_call(attend_forward_kernel, grid=(pairs,), out_shape=jax.ShapeD...  20.5 us

profile of v1, /device:TPU:0, one launch (start us, length us, event | category | flops | bytes accessed | tf_op | source)
XLA Modules:
  0.0 947.1 jit_solution(15029411907675648116)
XLA Ops:
  7.0 193.1 %shard_map.160 = bf16[2,32,304,768]{3,2,1,0:T(8,128)(2,1)S(1)} custom-call(bf16[2,304,768]{2,1,0:T(8,128)(2,1)S(1)} %concatenate.59.in_ref), custom_call_target="tpu_custom_call" | custom-call | tf_op jit(solution)/shard_map/pallas_call | solution.py:193
  200.1 10.2 %slice_bitcast_fusion = (bf16[32,304,768]{2,1,0:T(8,128)(2,1)}, bf16[32,304,768]{2,1,0:T(8,128)(2,1)}) fusion(bf16[2,32,304,768]{3,2,1,0:T(8,128)(2,1)S(1)} %shard_map.160), kind=kLoop, calls=%fused_computation | loop fusion | bytes 59768832 | tf_op jit(solution)/shard_map/squeeze | solution.py:581
  226.6 21.9 %shard_map.161 = bf16[1,4,256,1536]{3,2,1,0:T(8,128)(2,1)S(1)} custom-call(bf16[1,256,1536]{2,1,0:T(8,128)(2,1)S(1)} %slice_bitcast_fusion.3.in_ref), custom_call_target="tpu_custom_call" | custom-call | tf_op jit(solution)/shard_map/pallas_call | solution.py:193
  248.5 10.1 %shard_map.162 = bf16[256,768]{1,0:T(8,128)(2,1)S(1)} custom-call(bf16[256,2304]{1,0:T(8,128)(2,1)S(1)} %fusion.3.q_ref, bf16[1024,1536]{1,0:T(8,128)(2,1)S(1)} %bitcast.187, bf16[1024,1536]{1,0:T(8,128)(2,1)S(1)} %bitcast.188), custom_call_target="tpu_custom_call" | custom-call | tf_op jit(solution)/shard_map/pallas_call | solution.py:372
  261.3 6.6 fusion.107
  274.1 11.1 %fusion.7 = (bf16[256,3072]{1,0:T(8,128)(2,1)S(1)}, f32[256,3072]{1,0:T(8,128)}) fusion(f32[3072]{0:T(1024)S(1)} %add.213, bf16[768,3072]{1,0:T(8,128)(2,1)} %bitcast.219, f32[256,768]{1,0:T(8,128)S(1)} %get-tuple-element.122, f32[768]{0:T(1024)S(1)} %add.210, f32[768]{0:T(1024)S(1)} %mul.287, f32[256]{0:T(256)S(1)} %add_rsqrt_fusion.2, ...), kind=kOutput, calls=%fused_computation.25 | convolution fusion | flops 1260847104 | bytes 10244096 | tf_op jit(solution)/shard_map/dot_general | solution.py:21
  285.1 4.4 fusion.119
  300.9 21.9 %shard_map.163 = bf16[1,4,256,1536]{3,2,1,0:T(8,128)(2,1)S(1)} custom-call(bf16[1,256,1536]{2,1,0:T(8,128)(2,1)S(1)} %slice_bitcast_fusion.2.in_ref), custom_call_target="tpu_custom_call" | custom-call | tf_op jit(solution)/shard_map/pallas_call | solution.py:193
  322.9 10.4 %shard_map.164 = bf16[256,768]{1,0:T(8,128)(2,1)S(1)} custom-call(bf16[256,2304]{1,0:T(8,128)(2,1)S(1)} %fusion.4.q_ref, bf16[1024,1536]{1,0:T(8,128)(2,1)S(1)} %bitcast.191, bf16[1024,1536]{1,0:T(8,128)(2,1)S(1)} %bitcast.192), custom_call_target="tpu_custom_call" | custom-call | tf_op jit(solution)/shard_map/pallas_call | solution.py:372
  336.2 6.5 fusion.106
  348.9 11.1 %fusion.10 = (bf16[256,3072]{1,0:T(8,128)(2,1)}, f32[256,3072]{1,0:T(8,128)}) fusion(f32[3072]{0:T(1024)S(1)} %add.234, bf16[768,3072]{1,0:T(8,128)(2,1)} %bitcast.223, f32[256,768]{1,0:T(8,128)S(1)} %get-tuple-element.128, f32[768]{0:T(1024)S(1)} %add.231, f32[768]{0:T(1024)S(1)} %mul.302, f32[256]{0:T(256)S(1)} %add_rsqrt_fusion, ...), kind=kOutput, calls=%fused_computation.28 | convolution fusion | flops 1260847104 | bytes 10244096 | tf_op jit(solution)/shard_map/dot_general | solution.py:21
  360.7 5.1 fusion.38
  365.9 6.7 fusion.122
  376.2 16.4 %shard_map.165 = (bf16[256,768]{1,0:T(8,128)(2,1)S(1)}, bf16[1024,768]{1,0:T(8,128)(2,1)S(1)}, bf16[1024,768]{1,0:T(8,128)(2,1)S(1)}) custom-call(bf16[256,2304]{1,0:T(8,128)(2,1)S(1)} %copy-done.5, bf16[1024,1536]{1,0:T(8,128)(2,1)} %bitcast.193, bf16[1024,1536]{1,0:T(8,128)(2,1)} %bitcast.194, bf16[256,768]{1,0:T(8,128)(2,1)S(1)} %convolution_convert_fusion.9.go_ref), custom_call_target="tpu_custom_call" | custom-call | tf_op jit(solution)/shard_map/pallas_call | solution.py:389
  392.8 22.7 %shard_map.166 = bf16[256,1536]{1,0:T(8,128)(2,1)S(1)} custom-call(bf16[4,256,1536]{2,1,0:T(8,128)(2,1)S(1)} %bitcast.195), custom_call_target="tpu_custom_call" | custom-call | tf_op jit(solution)/shard_map/pallas_call | solution.py:317
  418.8 4.9 fusion.121
  427.8 16.6 %shard_map.167 = (bf16[256,768]{1,0:T(8,128)(2,1)S(1)}, bf16[1024,768]{1,0:T(8,128)(2,1)S(1)}, bf16[1024,768]{1,0:T(8,128)(2,1)S(1)}) custom-call(bf16[256,2304]{1,0:T(8,128)(2,1)S(1)} %copy-done.3, bf16[1024,1536]{1,0:T(8,128)(2,1)} %bitcast.189, bf16[1024,1536]{1,0:T(8,128)(2,1)} %bitcast.190, bf16[256,768]{1,0:T(8,128)(2,1)S(1)} %convolution_convert_fusion.8.go_ref), custom_call_target="tpu_custom_call" | custom-call | tf_op jit(solution)/shard_map/pallas_call | solution.py:389
  444.7 22.6 %shard_map.168 = bf16[256,1536]{1,0:T(8,128)(2,1)S(1)} custom-call(bf16[4,256,1536]{2,1,0:T(8,128)(2,1)S(1)} %bitcast.196), custom_call_target="tpu_custom_call" | custom-call | tf_op jit(solution)/shard_map/pallas_call | solution.py:317
  473.5 8.7 reshape.435
  482.2 4.9 copy.138
  488.7 3.8 convolution_convert_fusion.1
  492.5 10.0 %reshape.437 = bf16[32,24,4,768]{3,2,1,0:T(4,128)(2,1)} reshape(bf16[768,3072]{1,0:T(8,128)(2,1)} %convolution_convert_fusion.1) | data formatting | bytes 9437184 | tf_op jit(solution)/shard_map/reshape | solution.py:454
  502.5 5.5 copy.139
  513.6 72.4 %concatenate.70.in_ref = bf16[32,304,768]{2,1,0:T(8,128)(2,1)} concatenate(bf16[32,72,768]{2,1,0:T(8,128)(2,1)} %bitcast.211, bf16[32,24,768]{2,1,0:T(8,128)(2,1)} %bitcast.217, bf16[32,96,768]{2,1,0:T(8,128)(2,1)} %bitcast.201, bf16[32,96,768]{2,1,0:T(8,128)(2,1)} %bitcast.197, bf16[32,1,768]{2,1,0:T(2,128)(2,1)S(1)} %copy.144, bf16[32,15,768]{2,1,0:T(8,128)(2,1)S(1)} %broadcast.281), dimensions={1} | concatenate | bytes 29884416 | tf_op jit(solution)/shard_map/concatenate | solution.py:480
  586.0 119.9 %shard_map.170 = f32[304,768]{1,0:T(8,128)S(1)} custom-call(bf16[32,304,768]{2,1,0:T(8,128)(2,1)} %concatenate.70.in_ref), custom_call_target="tpu_custom_call" | custom-call | tf_op jit(solution)/shard_map/pallas_call | solution.py:317
  709.8 8.7 reshape.426
  718.5 5.0 copy.131
  725.0 3.8 convolution_convert_fusion.4
  728.8 10.0 %reshape.428 = bf16[32,24,4,768]{3,2,1,0:T(4,128)(2,1)} reshape(bf16[768,3072]{1,0:T(8,128)(2,1)} %convolution_convert_fusion.4) | data formatting | bytes 9437184 | tf_op jit(solution)/shard_map/reshape | solution.py:454
  738.8 5.5 copy.132
  749.7 72.4 %concatenate.67.in_ref = bf16[32,304,768]{2,1,0:T(8,128)(2,1)} concatenate(bf16[32,72,768]{2,1,0:T(8,128)(2,1)} %bitcast.212, bf16[32,24,768]{2,1,0:T(8,128)(2,1)} %bitcast.218, bf16[32,96,768]{2,1,0:T(8,128)(2,1)} %bitcast.202, bf16[32,96,768]{2,1,0:T(8,128)(2,1)} %bitcast.198, bf16[32,1,768]{2,1,0:T(2,128)(2,1)S(1)} %copy.137, bf16[32,15,768]{2,1,0:T(8,128)(2,1)S(1)} %broadcast.281), dimensions={1} | concatenate | bytes 29884416 | tf_op jit(solution)/shard_map/concatenate | solution.py:480
  822.2 118.5 %shard_map.169 = f32[304,768]{1,0:T(8,128)S(1)} custom-call(bf16[32,304,768]{2,1,0:T(8,128)(2,1)} %concatenate.67.in_ref), custom_call_target="tpu_custom_call" | custom-call | tf_op jit(solution)/shard_map/pallas_call | solution.py:317
  (375 shorter events, 92.8 us)
Async XLA Ops:
  211.4 85.8 %copy-start.41 = (f32[32,1,768]{2,0,1:T(8,128)}, f32[32,1,768]{2,0,1:T(8,128)S(1)}, u32[]{:S(2)}) copy-start(f32[32,1,768]{2,0,1:T(8,128)S(1)} %copy.154) | copy-start | bytes 294916
  226.5 32.1 %copy-start.2 = (bf16[256,2304]{1,0:T(8,128)(2,1)}, bf16[256,2304]{1,0:T(8,128)(2,1)S(1)}, u32[]{:S(2)}) copy-start(bf16[256,2304]{1,0:T(8,128)(2,1)S(1)} %fusion.3.q_ref) | copy-start | bytes 3538948
  261.2 24.0 %copy-start.10 = (f32[256,768]{1,0:T(8,128)}, f32[256,768]{1,0:T(8,128)S(1)}, u32[]{:S(2)}) copy-start(f32[256,768]{1,0:T(8,128)S(1)} %get-tuple-element.122) | copy-start | bytes 2359300
  273.8 11.3 %copy-start.50 = (f32[256]{0:T(256)}, f32[256]{0:T(256)S(1)}, u32[]{:S(2)}) copy-start(f32[256]{0:T(256)S(1)} %broadcast_multiply_fusion.10) | copy-start | bytes 3076
  274.1 11.1 %copy-start.60 = (f32[256]{0:T(256)}, f32[256]{0:T(256)S(1)}, u32[]{:S(2)}) copy-start(f32[256]{0:T(256)S(1)} %add_rsqrt_fusion.2) | copy-start | bytes 3076
  289.6 127.3 %copy-start.8 = (f32[256,768]{1,0:T(8,128)}, f32[256,768]{1,0:T(8,128)S(1)}, u32[]{:S(2)}) copy-start(f32[256,768]{1,0:T(8,128)S(1)} %get-tuple-element.126) | copy-start | bytes 2359300
  300.9 32.4 %copy-start.4 = (bf16[256,2304]{1,0:T(8,128)(2,1)}, bf16[256,2304]{1,0:T(8,128)(2,1)S(1)}, u32[]{:S(2)}) copy-start(bf16[256,2304]{1,0:T(8,128)(2,1)S(1)} %fusion.4.q_ref) | copy-start | bytes 3538948
  322.8 10.5 %copy-start.1 = (bf16[1,4,256,1536]{3,2,1,0:T(8,128)(2,1)}, bf16[1,4,256,1536]{3,2,1,0:T(8,128)(2,1)S(1)}, u32[]{:S(2)}) copy-start(bf16[1,4,256,1536]{3,2,1,0:T(8,128)(2,1)S(1)} %shard_map.163) | copy-start | bytes 9437188
  322.8 11.8 %copy-start.59 = (f32[768]{0:T(1024)S(1)}, f32[768]{0:T(1024)}, u32[]{:S(2)}) copy-start(f32[768]{0:T(1024)} %add.227) | copy-start | bytes 9220
  335.3 39.5 %copy-start.13 = (f32[256,768]{1,0:T(8,128)}, f32[256,768]{1,0:T(8,128)S(1)}, u32[]{:S(2)}) copy-start(f32[256,768]{1,0:T(8,128)S(1)} %get-tuple-element.128) | copy-start | bytes 2359300
  348.4 11.5 %copy-start.44 = (f32[768]{0:T(1024)}, f32[768]{0:T(1024)S(1)}, u32[]{:S(2)}) copy-start(f32[768]{0:T(1024)S(1)} %add.231) | copy-start | bytes 9220
  348.6 11.3 %copy-start.52 = (f32[256]{0:T(256)}, f32[256]{0:T(256)S(1)}, u32[]{:S(2)}) copy-start(f32[256]{0:T(256)S(1)} %broadcast_multiply_fusion.8) | copy-start | bytes 3076
  348.9 11.1 %copy-start.62 = (f32[256]{0:T(256)}, f32[256]{0:T(256)S(1)}, u32[]{:S(2)}) copy-start(f32[256]{0:T(256)S(1)} %add_rsqrt_fusion) | copy-start | bytes 3076
  348.9 11.1 %copy-start.46 = (f32[1,32,24]{1,2,0:T(8,128)S(1)}, f32[1,32,24]{1,2,0:T(8,128)}, u32[]{:S(2)}) copy-start(f32[1,32,24]{1,2,0:T(8,128)} %get-tuple-element.99) | copy-start | bytes 9220
  360.7 11.8 %slice-start.2 = ((s8[4718592]{0:T(1024)(128)(4,1)}), s8[4194304]{0:T(1024)(128)(4,1)S(1)}, s32[]{:S(2)}) async-start(s8[4718592]{0:T(1024)(128)(4,1)} %bitcast.224), calls=%async_computation.2 | async-start | bytes 8388608
  375.6 41.2 %copy-start.17 = (f32[256,768]{1,0:T(8,128)}, f32[256,768]{1,0:T(8,128)S(1)}, u32[]{:S(2)}) copy-start(f32[256,768]{1,0:T(8,128)S(1)} %get-tuple-element.69) | copy-start | bytes 2359300
  392.8 22.7 %copy-start.30 = (bf16[96,8,3,768]{3,1,2,0:T(8,128)(2,1)S(1)}, bf16[96,8,3,768]{3,1,2,0:T(8,128)(2,1)}, u32[]{:S(2)}) copy-start(bf16[96,8,3,768]{3,1,2,0:T(8,128)(2,1)} %copy.150) | copy-start | bytes 10616836
  392.8 22.7 %copy-start.49 = (f32[256]{0:T(256)S(1)}, f32[256]{0:T(256)}, u32[]{:S(2)}) copy-start(f32[256]{0:T(256)} %copy-done.48) | copy-start | bytes 3076
  392.8 22.7 %copy-start.56 = (f32[256]{0:T(256)S(1)}, f32[256]{0:T(256)}, u32[]{:S(2)}) copy-start(f32[256]{0:T(256)} %copy-done.55) | copy-start | bytes 3076
  426.9 42.3 %copy-start.15 = (f32[256,768]{1,0:T(8,128)}, f32[256,768]{1,0:T(8,128)S(1)}, u32[]{:S(2)}) copy-start(f32[256,768]{1,0:T(8,128)S(1)} %get-tuple-element.67) | copy-start | bytes 2359300
  444.4 22.9 %copy-start.58 = (f32[768]{0:T(1024)S(1)}, f32[768]{0:T(1024)}, u32[]{:S(2)}) copy-start(f32[768]{0:T(1024)} %copy-done.57) | copy-start | bytes 9220
  444.6 22.7 %copy-start.24 = (bf16[1,256,768]{2,1,0:T(8,128)(2,1)S(1)}, bf16[1,256,768]{2,1,0:T(8,128)(2,1)}, u32[]{:S(2)}) copy-start(bf16[1,256,768]{2,1,0:T(8,128)(2,1)} %param.9) | copy-start | bytes 1179652
  444.7 22.7 %copy-start.29 = (bf16[96,8,3,768]{3,1,2,0:T(8,128)(2,1)S(1)}, bf16[96,8,3,768]{3,1,2,0:T(8,128)(2,1)}, u32[]{:S(2)}) copy-start(bf16[96,8,3,768]{3,1,2,0:T(8,128)(2,1)} %copy.148) | copy-start | bytes 10616836
  444.7 22.7 %copy-start.66 = (f32[256]{0:T(256)S(1)}, f32[256]{0:T(256)}, u32[]{:S(2)}) copy-start(f32[256]{0:T(256)} %copy-done.65) | copy-start | bytes 3076
  444.7 22.7 %copy-start.73 = (f32[256]{0:T(256)S(1)}, f32[256]{0:T(256)}, u32[]{:S(2)}) copy-start(f32[256]{0:T(256)} %copy-done.72) | copy-start | bytes 3076
  586.0 120.7 %copy-start.74 = (f32[256]{0:T(256)S(1)}, f32[256]{0:T(256)}, u32[]{:S(2)}) copy-start(f32[256]{0:T(256)} %copy-done.72) | copy-start | bytes 3076
  586.0 120.7 %copy-start.76 = (f32[768]{0:T(1024)S(1)}, f32[768]{0:T(1024)}, u32[]{:S(2)}) copy-start(f32[768]{0:T(1024)} %copy-done.75) | copy-start | bytes 9220
  822.2 119.4 %copy-start.40 = (f32[1,24,768]{2,1,0:T(8,128)S(1)}, f32[1,24,768]{2,1,0:T(8,128)}, u32[]{:S(2)}) copy-start(f32[1,24,768]{2,1,0:T(8,128)} %get-tuple-element.88) | copy-start | bytes 221188
  822.2 120.1 %copy-start.36 = (f32[24,768]{1,0:T(8,128)S(1)}, f32[24,768]{1,0:T(8,128)}, u32[]{:S(2)}) copy-start(f32[24,768]{1,0:T(8,128)} %get-tuple-element.84) | copy-start | bytes 221188
  822.2 120.1 %copy-start.37 = (f32[24,768]{1,0:T(8,128)S(1)}, f32[24,768]{1,0:T(8,128)}, u32[]{:S(2)}) copy-start(f32[24,768]{1,0:T(8,128)} %get-tuple-element.85) | copy-start | bytes 221188
  822.2 120.1 %copy-start.38 = (f32[24,768]{1,0:T(8,128)S(1)}, f32[24,768]{1,0:T(8,128)}, u32[]{:S(2)}) copy-start(f32[24,768]{1,0:T(8,128)} %get-tuple-element.86) | copy-start | bytes 221188
  822.2 120.1 %copy-start.39 = (f32[24,768]{1,0:T(8,128)S(1)}, f32[24,768]{1,0:T(8,128)}, u32[]{:S(2)}) copy-start(f32[24,768]{1,0:T(8,128)} %get-tuple-element.87) | copy-start | bytes 221188
  (57 other events, 250.4 us)

commit v2 on v1

v2 whole, which is shorter than its diff:
```python
import functools

import jax
import jax.numpy as jnp
from jax import lax
from jax.experimental import pallas as pl
from jax.experimental.pallas import tpu as pltpu
from jax.sharding import PartitionSpec as P

D = 768
H = 12
HD = 64


eps_norm = 1e-05
root_half = 0.7071067811865476
inv_root_two_pi = 0.3989422804014327


def product(left, right):
    return jnp.dot(left, right, preferred_element_type=jnp.float32)


def product_left(left, right):
    return lax.dot_general(
        left, right, (((0,), (0,)), ((), ())), preferred_element_type=jnp.float32
    )


def product_right(left, right):
    return lax.dot_general(
        left, right, (((1,), (1,)), ((), ())), preferred_element_type=jnp.float32
    )


def norm_forward(rows, gain, shift):
    center = rows - jnp.mean(rows, axis=1, keepdims=True)
    inv_scale = lax.rsqrt(jnp.mean(center * center, axis=1, keepdims=True) + eps_norm)
    unit_rows = center * inv_scale
    return (unit_rows * gain + shift, unit_rows, inv_scale)


def norm_backward(upstream, unit_rows, inv_scale, gain):
    scaled = upstream * gain
    mean_plain = jnp.mean(scaled, axis=1, keepdims=True)
    mean_unit = jnp.mean(scaled * unit_rows, axis=1, keepdims=True)
    back = inv_scale * (scaled - mean_plain - unit_rows * mean_unit)
    return (back, jnp.sum(upstream * unit_rows, axis=0), jnp.sum(upstream, axis=0))


def gelu_slope(pre_gelu):
    cumulative = 0.5 * (1.0 + lax.erf(pre_gelu * root_half))
    density = jnp.exp(-0.5 * pre_gelu * pre_gelu) * inv_root_two_pi
    return cumulative + pre_gelu * density


def column_sums(rows):
    return jnp.sum(rows.astype(jnp.float32), axis=0)


def bit_of(index, weight):
    return lax.rem(lax.div(index, weight), 2)


def flip(index, weight):
    return index + weight - 2 * weight * bit_of(index, weight)


def bit_orders(clip_size, seq_size, with_clip=True):
    high = []
    weight = clip_size * seq_size // 2
    while weight >= seq_size and with_clip:
        high.append(weight)
        weight //= 2
    low = []
    weight = seq_size // 2
    while weight >= 1:
        low.append(weight)
        weight //= 2
    first = high + low
    if not high:
        return (first, first)
    second = high[:-1] + [low[0], high[-1]] + low[1:]
    return (first, second)


def spread(position, weights):
    total = 0
    for place, weight in enumerate(weights):
        total = total + weight * lax.rem(lax.div(position, 2**place), 2)
    return total


def partner_id(weight, seq_size):
    clip_at, seq_at = lax.axis_index("clip"), lax.axis_index("seq")
    if weight < seq_size:
        return {"clip": clip_at, "seq": flip(seq_at, weight)}
    return {"clip": flip(clip_at, weight // seq_size), "seq": seq_at}


def greet(weights, seq_size):
    barrier = pltpu.get_barrier_semaphore()
    for weight in weights:
        pl.semaphore_signal(
            barrier,
            inc=1,
            device_id=partner_id(weight, seq_size),
            device_id_type=pl.DeviceIdType.MESH,
        )
    pl.semaphore_wait(barrier, len(weights))


def round_up(value, step):
    return (value + step - 1) // step * step


def own_index(seq_size, with_clip):
    seq_at = lax.axis_index("seq")
    return lax.axis_index("clip") * seq_size + seq_at if with_clip else seq_at


def cube_gather(arrays, pieces, chains, sizes, with_clip, collective_id):
    clip_size, seq_size = sizes
    count = clip_size * seq_size if with_clip else seq_size
    orders = bit_orders(clip_size, seq_size, with_clip)
    stages = len(orders[0])
    last = max(chain[2] for chain in chains)

    def kernel(*refs):
        in_refs = refs[: len(arrays)]
        out_refs = refs[len(arrays) : len(arrays) + len(pieces)]
        own_sem, send_sem, recv_sem = refs[len(arrays) + len(pieces) :]
        greet(orders[0], seq_size)
        me = own_index(seq_size, with_clip)
        own = []
        for at, (array_at, index, _, _) in enumerate(pieces):
            copy = pltpu.make_async_copy(
                in_refs[array_at].at[index], out_refs[at].at[me], own_sem.at[at]
            )
            copy.start()
            own.append(copy)
        for copy in own:
            copy.wait()

        def transfer(at, stage, weight, source):
            return pltpu.make_async_remote_copy(
                src_ref=source,
                dst_ref=source,
                send_sem=send_sem.at[at, stage],
                recv_sem=recv_sem.at[at, stage],
                device_id=partner_id(weight, seq_size),
                device_id_type=pl.DeviceIdType.MESH,
            )

        def start_stage(chain, stage):
            order = orders[chain[1]]
            base = me
            for done in order[:stage]:
                base = base - done * bit_of(me, done)

            def one(position, carry):
                place = base + spread(position, order[:stage])
                for at in chain[0]:
                    transfer(at, stage, order[stage], out_refs[at].at[place]).start()
                return carry

            if stage == 0:
                one(0, 0)
            else:
                lax.fori_loop(0, 2**stage, one, 0)

        def wait_stage(chain, stage):
            for at in chain[0]:
                block = out_refs[at].at[pl.ds(0, 2**stage)]
                transfer(at, stage, orders[chain[1]][stage], block).wait()

        for tick in range(stages + last + 1):
            for chain in chains:
                stage = tick - chain[2]
                if 1 <= stage <= stages:
                    wait_stage(chain, stage - 1)
                if 0 <= stage < stages:
                    start_stage(chain, stage)

    return pl.pallas_call(
        kernel,
        out_shape=tuple(
            jax.ShapeDtypeStruct((count, rows, columns), jnp.bfloat16)
            for _, _, rows, columns in pieces
        ),
        in_specs=[pl.BlockSpec(memory_space=pl.ANY)] * len(arrays),
        out_specs=(pl.BlockSpec(memory_space=pl.ANY),) * len(pieces),
        scratch_shapes=[
            pltpu.SemaphoreType.DMA((len(pieces),)),
            pltpu.SemaphoreType.DMA((len(pieces), stages)),
            pltpu.SemaphoreType.DMA((len(pieces), stages)),
        ],
        compiler_params=pltpu.CompilerParams(
            collective_id=collective_id, has_side_effects=True, vmem_limit_bytes=16 * 2**20
        ),
    )(*arrays)


def cube_scatter(terms, chains, sizes, with_clip, collective_id, out_dtype):
    clip_size, seq_size = sizes
    count = terms[0].shape[0]
    orders = [order[::-1] for order in bit_orders(clip_size, seq_size, with_clip)]
    stages = len(orders[0])
    offsets = [sum(count // 2 ** (s + 1) for s in range(stage)) for stage in range(stages)]
    last = max(chain[2] for chain in chains)
    number = len(terms)

    def kernel(*refs):
        in_refs, out_refs = refs[:number], refs[number : 2 * number]
        totals, landeds = refs[2 * number : 3 * number], refs[3 * number : 4 * number]
        own_sem, send_sem, recv_sem = refs[4 * number :]
        greet(orders[0], seq_size)
        me = own_index(seq_size, with_clip)

        def transfer(at, stage, order, source, target):
            return pltpu.make_async_remote_copy(
                src_ref=source,
                dst_ref=target,
                send_sem=send_sem.at[at, stage],
                recv_sem=recv_sem.at[at, stage],
                device_id=partner_id(order[stage], seq_size),
                device_id_type=pl.DeviceIdType.MESH,
            )

        def first_place(order, position, mine):
            weight = order[0]
            bit = bit_of(me, weight) if mine else 1 - bit_of(me, weight)
            return weight * bit + spread(position, order[:0:-1])

        def bases(order, stage):
            base = 0
            for at in range(1, stage):
                base = base + count // 2 ** (at + 1) * bit_of(me, order[at])
            step = count // 2 ** (stage + 1)
            bit = bit_of(me, order[stage])
            return base + step * bit, base + step * (1 - bit)

        def start_stage(chain, stage):
            order = orders[chain[1]]
            blocks = count // 2 ** (stage + 1)
            if stage == 0:

                def one(position, carry):
                    for at in chain[0]:
                        source = in_refs[at].at[first_place(order, position, False)]
                        transfer(at, 0, order, source, landeds[at].at[position]).start()
                    return carry

                def load(position, carry):
                    for at in chain[0]:
                        source = in_refs[at].at[first_place(order, position, True)]
                        pltpu.make_async_copy(
                            source, totals[at].at[position], own_sem.at[at]
                        ).start()
                    return carry

                lax.fori_loop(0, blocks, one, 0)
                lax.fori_loop(0, blocks, load, 0)
            else:
                theirs = bases(order, stage)[1]
                for at in chain[0]:
                    source = totals[at].at[pl.ds(theirs, blocks)]
                    target = landeds[at].at[pl.ds(offsets[stage], blocks)]
                    transfer(at, stage, order, source, target).start()

        def finish_stage(chain, stage):
            order = orders[chain[1]]
            blocks = count // 2 ** (stage + 1)
            mine = bases(order, stage)[0] if stage else 0
            for at in chain[0]:
                source = (totals[at] if stage else in_refs[at]).at[pl.ds(0, blocks)]
                target = landeds[at].at[pl.ds(offsets[stage], blocks)]
                transfer(at, stage, order, source, target).wait()
                if stage == 0:
                    pltpu.make_async_copy(source, totals[at], own_sem.at[at]).wait()
                rows, columns = terms[at].shape[1:]
                high = rows if rows % 32 else 32
                tiles, wide = rows // high, D

                def add(step, carry, at=at, tiles=tiles, high=high, wide=wide, columns=columns):
                    position, tile = lax.div(step, tiles), lax.rem(step, tiles)
                    row = pl.ds(0, high)
                    if tiles > 1:
                        row = pl.ds(pl.multiple_of(tile * high, high), high)
                    for start in range(0, columns, wide):
                        part = pl.ds(start, wide)
                        summed = totals[at][mine + position, row, part].astype(
                            jnp.float32
                        ) + landeds[at][offsets[stage] + position, row, part].astype(jnp.float32)
                        if stage == stages - 1:
                            out_refs[at][row, part] = summed.astype(out_dtype)
                        else:
                            totals[at][mine + position, row, part] = summed.astype(jnp.bfloat16)
                    return carry

                lax.fori_loop(0, blocks * tiles, add, 0)

        for tick in range(stages + last + 1):
            for chain in chains:
                stage = tick - chain[2]
                if 1 <= stage <= stages:
                    finish_stage(chain, stage - 1)
                if 0 <= stage < stages:
                    start_stage(chain, stage)

    return pl.pallas_call(
        kernel,
        out_shape=tuple(jax.ShapeDtypeStruct(term.shape[1:], out_dtype) for term in terms),
        in_specs=[pl.BlockSpec(memory_space=pl.ANY)] * number,
        out_specs=(pl.BlockSpec(memory_space=pltpu.VMEM),) * number,
        scratch_shapes=[pltpu.VMEM((count // 2,) + t.shape[1:], t.dtype) for t in terms]
        + [pltpu.VMEM((count - 1,) + t.shape[1:], t.dtype) for t in terms]
        + [
            pltpu.SemaphoreType.DMA((number,)),
            pltpu.SemaphoreType.DMA((number, stages)),
            pltpu.SemaphoreType.DMA((number, stages)),
        ],
        compiler_params=pltpu.CompilerParams(
            collective_id=collective_id, has_side_effects=True, vmem_limit_bytes=56 * 2**20
        ),
    )(*terms)


def head_pair(ref, head):
    return ref[:, head * HD : (head + 1) * HD]


def probabilities(query, key):
    scores = product_right(query, key) * (HD ** (-0.5))
    powers = jnp.exp(scores - jnp.max(scores, axis=1, keepdims=True))
    return powers * (1.0 / jnp.sum(powers, axis=1, keepdims=True))


def attend_forward_kernel(q_ref, k_ref, v_ref, o_ref):
    outputs = []
    for head in range(2):
        probs = probabilities(head_pair(q_ref, head), head_pair(k_ref, head))
        outputs.append(product(probs.astype(jnp.bfloat16), head_pair(v_ref, head)))
    o_ref[...] = jnp.concatenate(outputs, axis=1).astype(o_ref.dtype)


def attend_backward_kernel(q_ref, k_ref, v_ref, go_ref, gq_ref, gk_ref, gv_ref):
    grads = ([], [], [])
    for head in range(2):
        query, key = head_pair(q_ref, head), head_pair(k_ref, head)
        value, upstream = head_pair(v_ref, head), head_pair(go_ref, head)
        probs = probabilities(query, key)
        grad_probs = product_right(upstream, value)
        inner = jnp.sum(grad_probs * probs, axis=1, keepdims=True)
        grad_scores = (probs * (grad_probs - inner)).astype(jnp.bfloat16)
        grads[0].append(product(grad_scores, key) * (HD ** (-0.5)))
        grads[1].append(product_left(grad_scores, query) * (HD ** (-0.5)))
        grads[2].append(product_left(probs.astype(jnp.bfloat16), upstream))
    for ref, pieces in zip((gq_ref, gk_ref, gv_ref), grads):
        ref[...] = jnp.concatenate(pieces, axis=1).astype(ref.dtype)


def attend_forward(projected, keys, values):
    rows, length = projected.shape[0], keys.shape[0]
    pairs = D // (2 * HD)
    return pl.pallas_call(
        attend_forward_kernel,
        grid=(pairs,),
        out_shape=jax.ShapeDtypeStruct((rows, D), jnp.bfloat16),
        in_specs=[
            pl.BlockSpec((rows, 2 * HD), lambda pair: (0, pair)),
            pl.BlockSpec((length, 2 * HD), lambda pair: (0, pair)),
            pl.BlockSpec((length, 2 * HD), lambda pair: (0, pair)),
        ],
        out_specs=pl.BlockSpec((rows, 2 * HD), lambda pair: (0, pair)),
        compiler_params=pltpu.CompilerParams(vmem_limit_bytes=40 * 2**20),
    )(projected, keys, values)


def attend_backward(projected, keys, values, grad_attended):
    rows, length = projected.shape[0], keys.shape[0]
    pairs = D // (2 * HD)
    return pl.pallas_call(
        attend_backward_kernel,
        grid=(pairs,),
        out_shape=(
            jax.ShapeDtypeStruct((rows, D), jnp.bfloat16),
            jax.ShapeDtypeStruct((length, D), jnp.bfloat16),
            jax.ShapeDtypeStruct((length, D), jnp.bfloat16),
        ),
        in_specs=[
            pl.BlockSpec((rows, 2 * HD), lambda pair: (0, pair)),
            pl.BlockSpec((length, 2 * HD), lambda pair: (0, pair)),
            pl.BlockSpec((length, 2 * HD), lambda pair: (0, pair)),
            pl.BlockSpec((rows, 2 * HD), lambda pair: (0, pair)),
        ],
        out_specs=(
            pl.BlockSpec((rows, 2 * HD), lambda pair: (0, pair)),
            pl.BlockSpec((length, 2 * HD), lambda pair: (0, pair)),
            pl.BlockSpec((length, 2 * HD), lambda pair: (0, pair)),
        ),
        compiler_params=pltpu.CompilerParams(vmem_limit_bytes=48 * 2**20),
    )(projected, keys, values, grad_attended)


def small_pad(small):
    rows = round_up((small.shape[-1] + D - 1) // D, 16)
    padding = [(0, 0)] * (small.ndim - 1) + [(0, rows * D - small.shape[-1])]
    return jnp.pad(small, padding).reshape(small.shape[:-1] + (rows, D))


def pack_small(norm_gains, shifts, mlp_bias):
    layers = norm_gains.shape[0]
    return small_pad(
        jnp.concatenate(
            [norm_gains.reshape(layers, -1), shifts.reshape(layers, -1), mlp_bias], axis=1
        )
    )


def unpack_layer(gathered, depth):
    count = gathered[0].shape[0]
    matrices = tuple(piece.reshape(-1, piece.shape[2]) for piece in gathered[:4])
    small = gathered[4].reshape(count, -1)[:, : 12 * depth].astype(jnp.float32)
    gains = small[:, : 2 * depth].reshape(count, 2, depth).transpose(1, 0, 2).reshape(2, D)
    shift_rows = small[:, 2 * depth : 8 * depth].reshape(count, 6, depth)
    shift_rows = shift_rows.transpose(1, 0, 2).reshape(6, D)
    bias_mlp = small[:, 8 * depth :].reshape(4 * D)
    return matrices + (gains, shift_rows, bias_mlp)


def by_owner(grad_terms, count):
    gains, shift_rows, bias = grad_terms[4:]
    depth = D // count
    small = jnp.concatenate(
        [
            gains.reshape(2, count, depth).transpose(1, 0, 2).reshape(count, -1),
            shift_rows.reshape(6, count, depth).transpose(1, 0, 2).reshape(count, -1),
            bias.reshape(count, -1),
        ],
        axis=1,
    ).astype(jnp.bfloat16)
    matrices = [
        term.astype(jnp.bfloat16).reshape(count, -1, term.shape[1]) for term in grad_terms[:4]
    ]
    return matrices + [small_pad(small)]


def unpack_shard(summed, depth):
    small = summed[4].reshape(-1)
    return tuple(summed[:4]) + (
        small[: 2 * depth].reshape(2, depth),
        small[2 * depth : 8 * depth].reshape(6, depth),
        small[8 * depth : 12 * depth],
    )


def layer_chains(layers):
    chains = []
    for place, layer in enumerate(layers):
        chains.append(([5 * layer, 5 * layer + 3], 0, place))
        chains.append(([5 * layer + 1, 5 * layer + 2, 5 * layer + 4], 1, place))
    return chains


def layer_forward(residual, weights, sizes, layer_index):
    w_attn_in, w_attn_out, w_mlp_in, w_mlp_out, gain_rows, shift_rows, bias_mlp = weights
    normed = norm_forward(residual, gain_rows[0], shift_rows[0])[0].astype(jnp.bfloat16)
    qkv_bias = jnp.concatenate([shift_rows[1], jnp.zeros_like(shift_rows[1]), shift_rows[2]])
    projected = (product(normed, w_attn_in) + qkv_bias).astype(jnp.bfloat16)
    rows = projected.shape[0]
    keys, values = cube_gather(
        (projected,),
        [(0, (slice(None), pl.ds(D * at, D)), rows, D) for at in (1, 2)],
        [([0], 0, 0), ([1], 0, 0)],
        sizes,
        False,
        2 + layer_index,
    )
    keys, values = keys.reshape(-1, D), values.reshape(-1, D)
    attended = attend_forward(projected, keys, values)
    middle = residual + product(attended, w_attn_out) + shift_rows[3]
    normed_two = norm_forward(middle, gain_rows[1], shift_rows[4])[0].astype(jnp.bfloat16)
    pre_gelu = product(normed_two, w_mlp_in) + bias_mlp
    hidden = jax.nn.gelu(pre_gelu, approximate=False).astype(jnp.bfloat16)
    result = middle + product(hidden, w_mlp_out) + shift_rows[5]
    saved = (residual, normed, projected, keys, values, attended, middle, normed_two, pre_gelu, hidden)
    return (result, saved)


def layer_backward(upstream, saved, weights, sizes, layer_index):
    w_attn_in, w_attn_out, w_mlp_in, w_mlp_out, gain_rows, shift_rows, bias_mlp = weights
    residual, normed, projected, keys, values, attended, middle, normed_two, pre_gelu, hidden = saved
    upstream_low = upstream.astype(jnp.bfloat16)
    grad_mlp_out = product_left(hidden, upstream_low)
    grad_bias_two = column_sums(upstream_low)
    grad_pre = (product_right(upstream_low, w_mlp_out) * gelu_slope(pre_gelu)).astype(jnp.bfloat16)
    grad_mlp_in = product_left(normed_two, grad_pre)
    grad_mlp_bias = column_sums(grad_pre)
    grad_normed_two = product_right(grad_pre, w_mlp_in)
    unit_two, scale_two = norm_forward(middle, gain_rows[1], shift_rows[4])[1:]
    back_two, grad_gain_two, grad_shift_two = norm_backward(
        grad_normed_two, unit_two, scale_two, gain_rows[1]
    )
    grad_middle = upstream + back_two
    middle_low = grad_middle.astype(jnp.bfloat16)
    grad_attn_out = product_left(attended, middle_low)
    grad_bias_out = column_sums(middle_low)
    grad_attended = product_right(middle_low, w_attn_out).astype(jnp.bfloat16)
    grad_queries, key_terms, value_terms = attend_backward(projected, keys, values, grad_attended)
    rows = grad_queries.shape[0]
    grad_keys, grad_values = cube_scatter(
        (key_terms.reshape(-1, rows, D), value_terms.reshape(-1, rows, D)),
        [([0], 0, 0), ([1], 0, 0)],
        sizes,
        False,
        4 + layer_index,
        jnp.bfloat16,
    )
    grad_projected = jnp.concatenate([grad_queries, grad_keys, grad_values], axis=1)
    grad_attn_in = product_left(normed, grad_projected)
    projected_sums = column_sums(grad_projected)
    grad_normed = product_right(grad_projected, w_attn_in)
    unit_one, scale_one = norm_forward(residual, gain_rows[0], shift_rows[0])[1:]
    back_one, grad_gain_one, grad_shift_one = norm_backward(
        grad_normed, unit_one, scale_one, gain_rows[0]
    )
    grad_residual = grad_middle + back_one
    grad_gains = jnp.stack([grad_gain_one, grad_gain_two])
    grad_shifts = jnp.stack(
        [
            grad_shift_one,
            projected_sums[:D],
            projected_sums[2 * D :],
            grad_bias_out,
            grad_shift_two,
            grad_bias_two,
        ]
    )
    grad_terms = (
        grad_attn_in,
        grad_attn_out,
        grad_mlp_in,
        grad_mlp_out,
        grad_gains,
        grad_shifts,
        grad_mlp_bias,
    )
    return (grad_residual, grad_terms)


def body(sizes, frames, out_grad, *params):
    layers, depth = params[0].shape[0], params[0].shape[1]
    count = sizes[0] * sizes[1]
    groups, frame_count, width = frames.shape
    residual = frames.astype(jnp.float32).reshape(groups * frame_count, width)
    arrays = tuple(params[:4]) + (pack_small(*params[4:]),)
    pieces = [
        (at, layer) + array.shape[1:] for layer in range(layers) for at, array in enumerate(arrays)
    ]
    gathered = cube_gather(arrays, pieces, layer_chains(range(layers)), sizes, True, 1)
    weights = [
        unpack_layer(gathered[5 * layer : 5 * layer + 5], depth) for layer in range(layers)
    ]
    saved_all = []
    for layer in range(layers):
        residual, saved = layer_forward(residual, weights[layer], sizes, layer)
        saved_all.append(saved)
    encoded = residual.astype(jnp.bfloat16).reshape(groups, frame_count, width)
    upstream = out_grad.astype(jnp.float32).reshape(groups * frame_count, width)
    terms = [None] * layers
    for layer in reversed(range(layers)):
        upstream, grad_terms = layer_backward(
            upstream, saved_all[layer], weights[layer], sizes, layer
        )
        terms[layer] = by_owner(grad_terms, count)
    if depth % 8 == 0:
        summed = cube_scatter(
            sum(terms, []), layer_chains(range(layers)), sizes, True, 6, jnp.float32
        )
    else:
        summed = ()
        for layer in range(layers):
            summed += tuple(
                cube_scatter(terms[layer], layer_chains([0]), sizes, True, 6 + layer, jnp.float32)
            )
    shards = [unpack_shard(summed[5 * layer : 5 * layer + 5], depth) for layer in range(layers)]
    outputs = tuple(jnp.stack(pieces) for pieces in zip(*shards))
    return (encoded, upstream.reshape(groups, frame_count, width)) + outputs


def solution(mesh):
    sizes = (mesh.shape["clip"], mesh.shape["seq"])
    specs = (
        P("clip", "seq", None),
        P("clip", "seq", None),
        P(None, ("clip", "seq"), None),
        P(None, ("clip", "seq"), None),
        P(None, ("clip", "seq"), None),
        P(None, ("clip", "seq"), None),
        P(None, None, ("clip", "seq")),
        P(None, None, ("clip", "seq")),
        P(None, ("clip", "seq")),
    )
    return jax.shard_map(
        functools.partial(body, sizes), mesh=mesh, in_specs=specs, out_specs=specs, check_vma=False
    )
```

time: 962 us -> 698 us (0.73)
  local copies, waits for them, and re-layouts: 274 us -> 62.5 us
  Pallas kernels: 574 us -> 524 us
    concatenate x3 -> x2, local copies, waits for them, and re-layouts: 148 us -> 1.2 us  [layer_backward(): jnp.concatenate([grad_queries, grad_keys, grad_values], axis=1)]
    pallas_call x7 -> x6, Pallas kernels: 521 us -> 471 us  [the longest x3 240 us: cube_gather(): pl.pallas_call(kernel, out_shape=tuple((jax.ShapeDtypeStruct((count, rows...]
    reshape x21 -> x12, local copies, waits for them, and re-layouts: 59.4 us -> 10.6 us  [the longest x2 5.76 us: unpack_layer(): small = gathered[4].reshape(count, -1)[:, :12 * depth].astype(jnp.float32)]
    slice x13 -> x4, local copies, waits for them, and re-layouts: 23.7 us -> 0.13 us  [unpack_layer(): bias_mlp = small[:, 8 * depth:].reshape(4 * D)]
    unnamed x196 -> x247, local copies, waits for them, and re-layouts: 15.2 us -> 33.2 us
    dot_general x8, matrix products: 39.1 us -> 26.9 us  [product(): return jnp.dot(left, right, preferred_element_type=jnp.float32)]
    squeeze x1 -> x0, local copies, waits for them, and re-layouts: 10.2 us -> none  [body(): weights = [unpack_layer(gathered[layer], depth) for layer in range(layers)]]
    transpose x6 -> x4, local copies, waits for them, and re-layouts: 10.3 us -> 0.36 us  [the longest x2 0.19 us: by_owner(): shift_rows.reshape(6, count, depth).transpose(1, 0, 2).reshape(count, -1)]
where the time goes in v2:
time: 698 us; the launch traced here: 689 us
  Pallas kernels  524 us (75%)
  matrix products  79.4 us (11%)
  local copies, waits for them, and re-layouts  62.5 us (9%)
  other arithmetic  20.4 us (3%)
    pallas_call x3, Pallas kernels, cube_gather(): pl.pallas_call(kernel, out_shape=tuple((jax.ShapeDtypeStruct((count, rows...  240 us
    pallas_call x3, Pallas kernels, cube_scatter(): pl.pallas_call(kernel, out_shape=tuple((jax.ShapeDtypeStruct(term.shape[1...  231 us
    unnamed x247, local copies, waits for them, and re-layouts  33.2 us
    pallas_call x2, Pallas kernels, attend_backward(): pl.pallas_call(attend_backward_kernel, grid=(pairs,), out_shape=(jax.Shap...  32.6 us
    dot_general x8, matrix products, product_right(): lax.dot_general(left, right, (((1,), (1,)), ((), ())), preferred_element_...  27 us
    dot_general x8, matrix products, product(): return jnp.dot(left, right, preferred_element_type=jnp.float32)  26.9 us
    dot_general x8, matrix products, product_left(): lax.dot_general(left, right, (((0,), (0,)), ((), ())), preferred_element_...  25.6 us
    pallas_call x2, Pallas kernels, attend_forward(): pl.pallas_call(attend_forward_kernel, grid=(pairs,), out_shape=jax.ShapeD...  20 us

profile of v2, /device:TPU:0, one launch (start us, length us, event | category | flops | bytes accessed | tf_op | source)
XLA Modules:
  0.0 689.1 jit_solution(3879824458056584235)
XLA Ops:
  10.9 196.4 %shard_map.160 = (bf16[32,24,2304]{2,1,0:T(8,128)(2,1)S(1)}, bf16[32,24,768]{2,1,0:T(8,128)(2,1)S(1)}, bf16[32,24,3072]{2,1,0:T(8,128)(2,1)S(1)}, bf16[32,96,768...) custom-call(bf16[2,24,2304]{2,1,0:T(8,128)(2,1)S(1)} %copy-done.19, ...), custom_call_target="tpu_custom_call" | custom-call | tf_op jit(solution)/shard_map/pallas_call | solution.py:185
  208.3 2.2 copy-done.21
  210.5 2.2 copy-done.22
  212.7 2.1 copy-done.23
  214.8 2.2 copy-done.24
  220.7 2.9 copy.104
  226.0 2.9 copy.105
  234.9 3.2 fusion.3.refs_0_.q_ref
  238.1 21.9 %shard_map.161 = (bf16[4,256,768]{2,1,0:T(8,128)(2,1)S(1)}, bf16[4,256,768]{2,1,0:T(8,128)(2,1)S(1)}) custom-call(bf16[256,2304]{1,0:T(8,128)(2,1)S(1)} %fusion.3.refs_0_.q_ref), custom_call_target="tpu_custom_call" | custom-call | tf_op jit(solution)/shard_map/pallas_call | solution.py:185
  260.1 10.0 %shard_map.162 = bf16[256,768]{1,0:T(8,128)(2,1)S(1)} custom-call(bf16[256,2304]{1,0:T(8,128)(2,1)S(1)} %fusion.3.refs_0_.q_ref, bf16[1024,768]{1,0:T(8,128)(2,1)S(1)} %bitcast.159, bf16[1024,768]{1,0:T(8,128)(2,1)S(1)} %bitcast.161), custom_call_target="tpu_custom_call" | custom-call | tf_op jit(solution)/shard_map/pallas_call | solution.py:366
  271.0 9.7 %fusion.7 = (bf16[256,3072]{1,0:T(8,128)(2,1)S(1)}, f32[256,3072]{1,0:T(8,128)}) fusion(f32[3072]{0:T(1024)S(1)} %add.213, bf16[768,3072]{1,0:T(8,128)(2,1)S(1)} %bitcast.178, f32[256,768]{1,0:T(8,128)S(1)} %get-tuple-element.149, f32[768]{0:T(1024)S(1)} %add.210, f32[768]{0:T(1024)S(1)} %mul.287, f32[256]{0:T(256)S(1)} %add_rsqrt_fusion.2, ...), kind=kOutput, calls=%fused_computation.23 | convolution fusion | flops 1260847104 | bytes 10244096 | tf_op jit(solution)/shard_map/dot_general | solution.py:21
  284.8 21.9 %shard_map.163 = (bf16[4,256,768]{2,1,0:T(8,128)(2,1)S(1)}, bf16[4,256,768]{2,1,0:T(8,128)(2,1)S(1)}) custom-call(bf16[256,2304]{1,0:T(8,128)(2,1)S(1)} %fusion.4.refs_0_.q_ref), custom_call_target="tpu_custom_call" | custom-call | tf_op jit(solution)/shard_map/pallas_call | solution.py:185
  306.7 10.0 %shard_map.164 = bf16[256,768]{1,0:T(8,128)(2,1)S(1)} custom-call(bf16[256,2304]{1,0:T(8,128)(2,1)S(1)} %fusion.4.refs_0_.q_ref, bf16[1024,768]{1,0:T(8,128)(2,1)S(1)} %bitcast.163, bf16[1024,768]{1,0:T(8,128)(2,1)S(1)} %bitcast.165), custom_call_target="tpu_custom_call" | custom-call | tf_op jit(solution)/shard_map/pallas_call | solution.py:366
  317.7 8.1 %fusion.10 = (bf16[256,3072]{1,0:T(8,128)(2,1)S(1)}, f32[256,3072]{1,0:T(8,128)S(1)}) fusion(f32[3072]{0:T(1024)S(1)} %copy-done.98, bf16[768,3072]{1,0:T(8,128)(2,1)S(1)} %bitcast.190, f32[256,768]{1,0:T(8,128)S(1)} %get-tuple-element.155, f32[768]{0:T(1024)S(1)} %copy-done.63, f32[768]{0:T(1024)S(1)} %mul.302, f32[256]{0:T(256)S(1)} %add_rsqrt_fusion, ...), kind=kOutput, calls=%fused_computation.26 | convolution fusion | flops 1260847104 | bytes 10244096 | tf_op jit(solution)/shard_map/dot_general | solution.py:21
  325.8 12.7 %fusion.105 = (bf16[3072]{0:T(1024)(128)(2,1)}, bf16[256,3072]{1,0:T(8,128)(2,1)S(1)}) fusion(f32[256,3072]{1,0:T(8,128)S(1)} %get-tuple-element.157, bf16[3072,768]{1,0:T(8,128)(2,1)S(1)} %bitcast.194, bf16[1,256,768]{2,1,0:T(8,128)(2,1)S(1)} %copy-done.46), kind=kOutput, calls=%fused_computation.223 | convolution fusion | flops 1216607232 | bytes 9836544 | tf_op jit(solution)/shard_map/dot_general | solution.py:31
  338.5 2.2 fusion.44
  340.7 3.0 multiply_reduce_fusion
  345.9 2.4 convert_reduce_fusion.3
  349.7 16.3 %shard_map.165 = (bf16[256,768]{1,0:T(8,128)(2,1)S(1)}, bf16[1024,768]{1,0:T(8,128)(2,1)S(1)}, bf16[1024,768]{1,0:T(8,128)(2,1)S(1)}) custom-call(bf16[256,2304]{1,0:T(8,128)(2,1)S(1)} %fusion.4.refs_0_.q_ref, bf16[1024,768]{1,0:T(8,128)(2,1)} %bitcast.164, bf16[1024,768]{1,0:T(8,128)(2,1)} %bitcast.166, bf16[256,768]{1,0:T(8,128)(2,1)S(1)} %convolution_convert_fusion.9.go_ref), custom_call_target="tpu_custom_call" | custom-call | tf_op jit(solution)/shard_map/pallas_call | solution.py:383
  369.0 23.7 %shard_map.166 = (bf16[256,768]{1,0:T(8,128)(2,1)}, bf16[256,768]{1,0:T(8,128)(2,1)}) custom-call(bf16[4,256,768]{2,1,0:T(8,128)(2,1)} %bitcast.171, bf16[4,256,768]{2,1,0:T(8,128)(2,1)} %bitcast.172), custom_call_target="tpu_custom_call" | custom-call | tf_op jit(solution)/shard_map/pallas_call | solution.py:311
  399.1 4.1 multiply_reduce_fusion.1
  405.4 2.4 fusion.104
  412.9 16.3 %shard_map.167 = (bf16[256,768]{1,0:T(8,128)(2,1)S(1)}, bf16[1024,768]{1,0:T(8,128)(2,1)S(1)}, bf16[1024,768]{1,0:T(8,128)(2,1)S(1)}) custom-call(bf16[256,2304]{1,0:T(8,128)(2,1)S(1)} %fusion.3.refs_0_.q_ref, bf16[1024,768]{1,0:T(8,128)(2,1)} %bitcast.160, bf16[1024,768]{1,0:T(8,128)(2,1)} %bitcast.162, bf16[256,768]{1,0:T(8,128)(2,1)S(1)} %convolution_convert_fusion.8.go_ref), custom_call_target="tpu_custom_call" | custom-call | tf_op jit(solution)/shard_map/pallas_call | solution.py:383
  431.7 23.8 %shard_map.168 = (bf16[256,768]{1,0:T(8,128)(2,1)}, bf16[256,768]{1,0:T(8,128)(2,1)}) custom-call(bf16[4,256,768]{2,1,0:T(8,128)(2,1)} %bitcast.173, bf16[4,256,768]{2,1,0:T(8,128)(2,1)} %bitcast.174), custom_call_target="tpu_custom_call" | custom-call | tf_op jit(solution)/shard_map/pallas_call | solution.py:311
  462.7 2.1 fusion.59
  469.8 4.4 convolution_convert_fusion.2
  474.3 3.1 convolution_convert_fusion.5
  477.4 3.7 convolution_convert_fusion.4
  481.2 3.8 convolution_convert_fusion.1
  485.0 3.7 convolution_convert_fusion.3
  488.7 3.9 convolution_convert_fusion
  492.5 183.6 %shard_map.169 = (f32[24,2304]{1,0:T(8,128)}, f32[24,768]{1,0:T(8,128)}, f32[24,3072]{1,0:T(8,128)}, f32[96,768]{1,0:T(8,128)}, f32[16,768]{1,0:T(8,128)}, /*ind...) custom-call(bf16[32,24,2304]{2,1,0:T(8,128)(2,1)} %bitcast.204, ...), custom_call_target="tpu_custom_call" | custom-call | tf_op jit(solution)/shard_map/pallas_call | solution.py:311
  (392 shorter events, 75.5 us)
Async XLA Ops:
  2.5 232.4 %copy-start.77 = (f32[256]{0:T(256)}, f32[256]{0:T(256)S(1)}, u32[]{:S(2)}) copy-start(f32[256]{0:T(256)S(1)} %broadcast_multiply_fusion.11) | copy-start | bytes 3076
  3.8 231.1 %copy-start.87 = (f32[256]{0:T(256)}, f32[256]{0:T(256)S(1)}, u32[]{:S(2)}) copy-start(f32[256]{0:T(256)S(1)} %add_rsqrt_fusion.3) | copy-start | bytes 3076
  225.3 45.6 %copy-start.59 = (f32[768]{0:T(1024)}, f32[768]{0:T(1024)S(1)}, u32[]{:S(2)}) copy-start(f32[768]{0:T(1024)S(1)} %add.210) | copy-start | bytes 9220
  226.0 12.1 %copy-start.61 = (f32[768]{0:T(1024)}, f32[768]{0:T(1024)S(1)}, u32[]{:S(2)}) copy-start(f32[768]{0:T(1024)S(1)} %add.200) | copy-start | bytes 9220
  238.1 32.8 %slice-start = ((s8[4718592]{0:T(1024)(128)(4,1)}), s8[4194304]{0:T(1024)(128)(4,1)S(1)}, s32[]{:S(2)}) async-start(s8[4718592]{0:T(1024)(128)(4,1)} %bitcast.176), calls=%async_computation | async-start | bytes 8388608
  260.1 10.9 %slice-start.1 = ((s8[4718592]{0:T(1024)(128)(4,1)}), s8[524288]{0:T(1024)(128)(4,1)S(1)}, s32[]{:S(2)}) async-start(s8[4718592]{0:T(1024)(128)(4,1)} %bitcast.176), calls=%async_computation.1 | async-start | bytes 1048576
  270.1 10.7 %copy-start.7 = (bf16[256,768]{1,0:T(8,128)(2,1)}, bf16[256,768]{1,0:T(8,128)(2,1)S(1)}, u32[]{:S(2)}) copy-start(bf16[256,768]{1,0:T(8,128)(2,1)S(1)} %shard_map.162) | copy-start | bytes 1179652
  270.1 10.7 %slice-start.4 = ((s8[4718592]{0:T(1024)(128)(4,1)}), s8[4194304]{0:T(1024)(128)(4,1)S(1)}, s32[]{:S(2)}) async-start(s8[4718592]{0:T(1024)(128)(4,1)} %bitcast.182), calls=%async_computation.4 | async-start | bytes 8388608
  282.3 34.4 %copy-start.29 = (f32[256,768]{1,0:T(8,128)}, f32[256,768]{1,0:T(8,128)S(1)}, u32[]{:S(2)}) copy-start(f32[256,768]{1,0:T(8,128)S(1)} %get-tuple-element.153) | copy-start | bytes 2359300
  283.6 34.1 %slice-start.8 = ((s8[4718592]{0:T(1024)(128)(4,1)}), s8[4194304]{0:T(1024)(128)(4,1)S(1)}, s32[]{:S(2)}) async-start(s8[4718592]{0:T(1024)(128)(4,1)} %bitcast.188), calls=%async_computation.8 | async-start | bytes 8388608
  284.7 32.0 %copy-start.5 = (bf16[32,24,768]{2,1,0:T(8,128)(2,1)S(1)}, bf16[32,24,768]{2,1,0:T(8,128)(2,1)}, u32[]{:S(2)}) copy-start(bf16[32,24,768]{2,1,0:T(8,128)(2,1)} %copy-done.4) | copy-start | bytes 3538948
  284.8 32.0 %copy-start.89 = (f32[768]{0:T(1024)S(1)}, f32[768]{0:T(1024)}, u32[]{:S(2)}) copy-start(f32[768]{0:T(1024)} %add.227) | copy-start | bytes 9220
  306.7 10.7 %copy-start.2 = (bf16[4,256,768]{2,1,0:T(8,128)(2,1)}, bf16[4,256,768]{2,1,0:T(8,128)(2,1)S(1)}, u32[]{:S(2)}) copy-start(bf16[4,256,768]{2,1,0:T(8,128)(2,1)S(1)} %get-tuple-element.52) | copy-start | bytes 4718596
  306.7 10.7 %copy-start.3 = (bf16[4,256,768]{2,1,0:T(8,128)(2,1)}, bf16[4,256,768]{2,1,0:T(8,128)(2,1)S(1)}, u32[]{:S(2)}) copy-start(bf16[4,256,768]{2,1,0:T(8,128)(2,1)S(1)} %get-tuple-element.53) | copy-start | bytes 4718596
  306.7 10.9 %slice-start.9 = ((s8[4718592]{0:T(1024)(128)(4,1)}), s8[524288]{0:T(1024)(128)(4,1)S(1)}, s32[]{:S(2)}) async-start(s8[4718592]{0:T(1024)(128)(4,1)} %bitcast.188), calls=%async_computation.9 | async-start | bytes 1048576
  306.7 10.9 %copy-start.63 = (f32[768]{0:T(1024)S(1)}, f32[768]{0:T(1024)}, u32[]{:S(2)}) copy-start(f32[768]{0:T(1024)} %add.231) | copy-start | bytes 9220
  306.7 10.9 %copy-start.98 = (f32[3072]{0:T(1024)S(1)}, f32[3072]{0:T(1024)}, u32[]{:S(2)}) copy-start(f32[3072]{0:T(1024)} %add.234) | copy-start | bytes 36868
  317.4 23.3 %copy-start.34 = (f32[256,768]{1,0:T(8,128)}, f32[256,768]{1,0:T(8,128)S(1)}, u32[]{:S(2)}) copy-start(f32[256,768]{1,0:T(8,128)S(1)} %get-tuple-element.155) | copy-start | bytes 2359300
  317.4 23.3 %copy-start.82 = (f32[256]{0:T(256)}, f32[256]{0:T(256)S(1)}, u32[]{:S(2)}) copy-start(f32[256]{0:T(256)S(1)} %broadcast_multiply_fusion.8) | copy-start | bytes 3076
  317.7 23.0 %copy-start.93 = (f32[256]{0:T(256)}, f32[256]{0:T(256)S(1)}, u32[]{:S(2)}) copy-start(f32[256]{0:T(256)S(1)} %add_rsqrt_fusion) | copy-start | bytes 3076
  325.8 12.7 %copy-start.50 = (bf16[256,3072]{1,0:T(8,128)(2,1)}, bf16[256,3072]{1,0:T(8,128)(2,1)S(1)}, u32[]{:S(2)}) copy-start(bf16[256,3072]{1,0:T(8,128)(2,1)S(1)} %get-tuple-element.156) | copy-start | bytes 4718596
  325.8 12.7 %copy-start.100 = (f32[768]{0:T(1024)S(1)}, f32[768]{0:T(1024)}, u32[]{:S(2)}) copy-start(f32[768]{0:T(1024)} %add.238) | copy-start | bytes 9220
  369.0 30.1 %copy-start.30 = (f32[256,768]{1,0:T(8,128)S(1)}, f32[256,768]{1,0:T(8,128)}, u32[]{:S(2)}) copy-start(f32[256,768]{1,0:T(8,128)} %copy-done.29) | copy-start | bytes 2359300
  369.0 27.8 %copy-start.16 = (bf16[256,768]{1,0:T(8,128)(2,1)S(1)}, bf16[256,768]{1,0:T(8,128)(2,1)}, u32[]{:S(2)}) copy-start(bf16[256,768]{1,0:T(8,128)(2,1)} %copy-done.15) | copy-start | bytes 1179652
  412.9 45.4 %copy-start.75 = (bf16[1,32,24]{2,1,0:T(8,128)(2,1)S(1)}, bf16[1,32,24]{2,1,0:T(8,128)(2,1)}, u32[]{:S(2)}) copy-start(bf16[1,32,24]{2,1,0:T(8,128)(2,1)} %stack.122) | copy-start | bytes 4612
  431.7 26.9 %copy-start.45 = (bf16[256,2304]{1,0:T(8,128)(2,1)S(1)}, bf16[256,2304]{1,0:T(8,128)(2,1)}, u32[]{:S(2)}) copy-start(bf16[256,2304]{1,0:T(8,128)(2,1)} %copy-done.44) | copy-start | bytes 3538948
  431.7 28.1 %copy-start.70 = (bf16[1,32,24]{2,1,0:T(8,128)(2,1)S(1)}, bf16[1,32,24]{2,1,0:T(8,128)(2,1)}, u32[]{:S(2)}) copy-start(bf16[1,32,24]{2,1,0:T(8,128)(2,1)} %stack.127) | copy-start | bytes 4612
  431.7 28.2 %copy-start.71 = (bf16[1,32,24]{2,1,0:T(8,128)(2,1)S(1)}, bf16[1,32,24]{2,1,0:T(8,128)(2,1)}, u32[]{:S(2)}) copy-start(bf16[1,32,24]{2,1,0:T(8,128)(2,1)} %stack.128) | copy-start | bytes 4612
  431.7 28.2 %copy-start.69 = (bf16[1,32,24]{2,1,0:T(8,128)(2,1)S(1)}, bf16[1,32,24]{2,1,0:T(8,128)(2,1)}, u32[]{:S(2)}) copy-start(bf16[1,32,24]{2,1,0:T(8,128)(2,1)} %stack.129) | copy-start | bytes 4612
  431.7 28.4 %copy-start.67 = (bf16[32,96]{1,0:T(8,128)(2,1)S(1)}, bf16[32,96]{1,0:T(8,128)(2,1)}, u32[]{:S(2)}) copy-start(bf16[32,96]{1,0:T(8,128)(2,1)} %reshape.440) | copy-start | bytes 18436
  676.1 11.7 %copy-start.57 = (f32[96,768]{1,0:T(8,128)S(1)}, f32[96,768]{1,0:T(8,128)}, u32[]{:S(2)}) copy-start(f32[96,768]{1,0:T(8,128)} %get-tuple-element.73) | copy-start | bytes 884740
  676.1 11.7 %copy-start.58 = (f32[96,768]{1,0:T(8,128)S(1)}, f32[96,768]{1,0:T(8,128)}, u32[]{:S(2)}) copy-start(f32[96,768]{1,0:T(8,128)} %get-tuple-element.74) | copy-start | bytes 884740
  (82 other events, 306.2 us)
